TPU v7x, 256 devices: a whole 4x4x8 slice. The times are simulated.
256 devices in a mesh: wide: 32 (over z_lo, y, core), narrow: 8 (over z_hi, x).
Axes of the slice: x: 4, y: 4, z: 8 (z_hi: 2, z_lo: 4; z = z_hi * 4 + z_lo), core: 2. Of those that a mesh axis runs over, the one named last changes fastest.
Arguments:
- divergence: float32 [256, 256, 256], P('wide', 'narrow'), may hold values from -5 to 5
- screening: float32 [256, 256, 256], P('wide', 'narrow'), may hold values from 0.0001 to 0.1
Outputs:
- solution_field: float32 [256, 256, 256], P('wide', 'narrow')
- residual: float32 [256, 256, 256], P('wide', 'narrow')
All inputs are finite; a program needn't handle non-finite values.
Results may differ from a plain program's by a relative error of at most 0.0003.
Values sent between devices are 32-bit elements; how exact they have to be, the bound alone decides.
A program may use at most 128 MiB of HBM per device.

v0:
```python
import jax
import jax.numpy as jnp
from jax import lax
from jax.sharding import PartitionSpec as P

SWEEPS = 2


relaxation = 0.8


def padded_2(block, sides, width):
    for axis, dim in sides:
        count = lax.axis_size(axis)
        forward = [(i, i + 1) for i in range(count - 1)]
        backward = [(target, source) for source, target in forward]
        low = lax.ppermute(
            lax.slice_in_dim(block, block.shape[dim] - width, None, axis=dim), axis, forward
        )
        high = lax.ppermute(lax.slice_in_dim(block, 0, width, axis=dim), axis, backward)
        block = jnp.concatenate([low, block, high], axis=dim)
    return block


def neighbour_sum(padded):
    summed = padded[2:, 1:-1, 1:-1] + padded[:-2, 1:-1, 1:-1]
    summed = summed + padded[1:-1, 2:, 1:-1] + padded[1:-1, :-2, 1:-1]
    return summed + padded[1:-1, 1:-1, 2:] + padded[1:-1, 1:-1, :-2]


def coarsen(values):
    extent = values.shape
    blocks = values.reshape(extent[0] // 2, 2, extent[1] // 2, 2, extent[2] // 2, 2)
    return 0.5 * jnp.sum(blocks, axis=(1, 3, 5))


def refine(values):
    return jnp.repeat(jnp.repeat(jnp.repeat(values, 2, axis=0), 2, axis=1), 2, axis=2)


def sine_table(count):
    ladder = jnp.arange(count, dtype=jnp.float32) + 1.0
    return jnp.sin(jnp.pi * ladder[:, None] * ladder[None, :] / (count + 1.0))


def sine_eigen(count):
    ladder = jnp.arange(count, dtype=jnp.float32) + 1.0
    return 2.0 - 2.0 * jnp.cos(jnp.pi * ladder / (count + 1.0))


def transform_all(values, tables):
    first, second, third = tables
    values = jnp.einsum("ai,ijk->ajk", first, values, precision=lax.Precision.HIGHEST)
    values = jnp.einsum("bj,ajk->abk", second, values, precision=lax.Precision.HIGHEST)
    return jnp.einsum("ck,abk->abc", third, values, precision=lax.Precision.HIGHEST)


def coarse_solve(source, screen):
    extent = source.shape
    tables = (sine_table(extent[0]), sine_table(extent[1]), sine_table(extent[2]))
    shift_mean = jnp.mean(screen)
    spectrum = (
        shift_mean
        + sine_eigen(extent[0])[:, None, None]
        + sine_eigen(extent[1])[None, :, None]
        + sine_eigen(extent[2])[None, None, :]
    )
    scaled = transform_all(source, tables) / spectrum
    factor = 2.0 / (extent[0] + 1.0) * (2.0 / (extent[1] + 1.0)) * (2.0 / (extent[2] + 1.0))
    return factor * transform_all(scaled, tables)


def update(iterate, source, screen, summed):
    return iterate + relaxation * (source - ((6.0 + screen) * iterate - summed)) / (6.0 + screen)


def pencil_neighbours(iterate):
    widened = padded_2(iterate, (("wide", 0), ("narrow", 1)), 1)
    return neighbour_sum(jnp.pad(widened, ((0, 0), (0, 0), (1, 1))))


def slab_neighbours(iterate):
    widened = padded_2(iterate, (("wide", 0),), 1)
    return neighbour_sum(jnp.pad(widened, ((0, 0), (1, 1), (1, 1))))


def post_smooth(iterate, source, screen):
    for sweep_index in range(SWEEPS):
        iterate = update(iterate, source, screen, pencil_neighbours(iterate))
    return iterate


def per_device(divergence, screening):
    wide_rank = lax.axis_index("wide")
    narrow_rank = lax.axis_index("narrow")
    sources = [divergence]
    screens = [screening]
    smoothed = []
    for level_index in range(2):
        source = sources[level_index]
        screen = screens[level_index]
        iterate = relaxation * source / (6.0 + screen)
        iterate = update(iterate, source, screen, pencil_neighbours(iterate))
        smoothed.append(iterate)
        remainder = source - ((6.0 + screen) * iterate - pencil_neighbours(iterate))
        sources.append(coarsen(remainder))
        screens.append(coarsen(screen) * 0.25)
    pencil_cols = sources[2].shape[1]
    source, screen = (
        lax.all_gather(sources[2], "narrow", axis=1, tiled=True),
        lax.all_gather(screens[2], "narrow", axis=1, tiled=True),
    )
    iterate = relaxation * source / (6.0 + screen)
    iterate = update(iterate, source, screen, slab_neighbours(iterate))
    level_two = iterate
    remainder = source - ((6.0 + screen) * iterate - slab_neighbours(iterate))
    part_source = coarsen(remainder)
    part_screen = coarsen(screen) * 0.25
    coarse_source, coarse_screen = (
        lax.all_gather(part_source, "wide", axis=0, tiled=True),
        lax.all_gather(part_screen, "wide", axis=0, tiled=True),
    )
    coarse = coarse_solve(coarse_source, coarse_screen)
    coarse_rows = level_two.shape[0] // 2
    own_block = lax.dynamic_slice_in_dim(coarse, wide_rank * coarse_rows, coarse_rows, 0)
    iterate = level_two + refine(own_block)
    for sweep_index in range(SWEEPS):
        iterate = update(iterate, source, screen, slab_neighbours(iterate))
    iterate = lax.dynamic_slice_in_dim(iterate, narrow_rank * pencil_cols, pencil_cols, 1)
    for level_index in (1, 0):
        iterate = post_smooth(
            smoothed[level_index] + refine(iterate), sources[level_index], screens[level_index]
        )
    remainder = divergence - ((6.0 + screening) * iterate - pencil_neighbours(iterate))
    return (iterate, remainder)


def solution(mesh):
    in_specs = (P("wide", "narrow", None), P("wide", "narrow", None))
    out_specs = (P("wide", "narrow", None), P("wide", "narrow", None))
    return jax.shard_map(
        per_device, mesh=mesh, in_specs=in_specs, out_specs=out_specs, check_vma=False
    )
```

profile of v0, /device:TPU:160, one launch (start us, length us, event | category | flops | bytes accessed | tf_op | source)
XLA Modules:
  0.0 596.5 jit_solution(15365223173667972325)
XLA Ops:
  6.5 5.8 collective-permute-start
  17.4 3.7 collective-permute-start.2
  23.3 9.5 %collective-permute-done.3 = f32[10,1,256]{2,1,0:T(1,128)S(1)} collective-permute-done((f32[10,1,256]{2,1,0:T(1,128)S(1)}, f32[10,1,256]{2,1,0:T(1,128)S(1)}, u32[]{:S(2)}, u32[]{:S(2)}) %collective-permute-start.3) | collective-permute-done | bytes 10272 | tf_op jit(solution)/shard_map/ppermute | solution.py:17
  34.2 2.3 copy.281
  36.6 2.3 copy.282
  39.7 2.5 copy.229
  42.2 5.3 fusion.6
  50.2 5.8 collective-permute-start.4
  63.6 4.1 collective-permute-start.7
  67.8 18.8 %reshape.136 = f32[4,2,16,2,128,2]{5,4,3,2,1,0:T(8,128)} reshape(f32[8,32,256]{2,1,0:T(8,128)} %param.3) | data formatting | bytes 524288 | tf_op jit(solution)/shard_map/reshape | solution.py:33
  86.6 7.0 %reduce_sum.78 = f32[4,16,128]{2,1,0:T(8,128)S(1)} reduce(f32[4,2,16,2,128,2]{5,4,3,2,1,0:T(8,128)} %reshape.136, f32[]{:T(128)} %constant.22.clone.1), dimensions={1,3,5}, to_apply=%region_1.2 | reduce | flops 57344 | bytes 294916 | tf_op jit(solution)/shard_map/reduce_sum | solution.py:34
  95.2 2.3 copy.283
  101.2 3.5 copy.236
  104.8 4.9 fusion.10
  111.2 18.1 %reshape.135 = f32[4,2,16,2,128,2]{5,4,3,2,1,0:T(8,128)} reshape(f32[8,32,256]{2,1,0:T(8,128)S(1)} %copy.238) | data formatting | bytes 524288 | tf_op jit(solution)/shard_map/reshape | solution.py:33
  129.3 7.0 %reduce_sum.77 = f32[4,16,128]{2,1,0:T(8,128)S(1)} reduce(f32[4,2,16,2,128,2]{5,4,3,2,1,0:T(8,128)} %reshape.135, f32[]{:T(128)} %constant.22.clone.1), dimensions={1,3,5}, to_apply=%region_0.1 | reduce | flops 57344 | bytes 294916 | tf_op jit(solution)/shard_map/reduce_sum | solution.py:34
  136.3 5.3 collective-permute-start.8
  143.6 5.1 collective-permute-done.9
  148.7 8.2 %collective-permute-start.10 = (f32[6,1,128]{2,1,0:T(1,128)S(1)}, f32[6,1,128]{2,1,0:T(1,128)S(1)}, u32[]{:S(2)}, u32[]{:S(2)}) collective-permute-start(f32[6,1,128]{2,1,0:T(1,128)S(1)} %get-tuple-element.65), channel_id=1, source_target_pairs={{1,0},{2,1},{3,2},{4,3},{5,4},{6,5},{7,6},{9,8},{10,9},{11,10},{12... | collective-permute-start | bytes 9224 | tf_op jit(solution)/shard_map/ppermute | solution.py:20
  158.9 3.4 mul.260
  164.1 4.3 collective-permute-done.11
  170.6 2.4 collective-permute-start.13
  173.0 4.6 collective-permute-done.13
  177.7 5.6 collective-permute-start.14
  185.3 43.8 %all_gather.13 = f32[2,64,64]{2,1,0:T(8,128)S(1)} all-gather(f32[2,8,64]{2,1,0:T(8,128)S(1)} %broadcast_multiply_fusion.3), channel_id=1, replica_groups=mesh['wide'=32,'narrow'=8] {'narrow'}, dimensions={1}, use_global_device_ids=true | all-gather | bytes 36864 | tf_op jit(solution)/shard_map/all_gather | solution.py:111
  229.3 3.4 reshape.137
  234.5 43.8 %all_gather.12 = f32[2,64,64]{2,1,0:T(8,128)S(1)} all-gather(f32[2,8,64]{2,1,0:T(8,128)S(1)} %broadcast_multiply_fusion.4), channel_id=1, replica_groups=mesh['wide'=32,'narrow'=8] {'narrow'}, dimensions={1}, use_global_device_ids=true | all-gather | bytes 36864 | tf_op jit(solution)/shard_map/all_gather | solution.py:110
  280.5 2.4 collective-permute-start.17
  283.0 4.9 collective-permute-done.17
  290.6 2.4 collective-permute-start.19
  293.1 4.9 collective-permute-done.19
  298.8 2.9 reduce_sum.82
  303.1 31.8 %all-gather = f32[1024,32]{1,0:T(8,128)S(1)} all-gather(f32[32,32]{1,0:T(8,128)S(1)} %broadcast_multiply_fusion.2), channel_id=2, replica_groups=mesh['wide'=32,'narrow'=8] {'wide'}, dimensions={0}, use_global_device_ids=true | all-gather | bytes 135168 | tf_op jit(solution)/shard_map/all_gather | solution.py:120
  341.5 40.5 %all-gather.1 = f32[1024,32]{1,0:T(8,128)} all-gather(f32[32,32]{1,0:T(8,128)S(1)} %broadcast_multiply_fusion.1), channel_id=3, replica_groups=mesh['wide'=32,'narrow'=8] {'wide'}, dimensions={0}, use_global_device_ids=true | all-gather | bytes 135168 | tf_op jit(solution)/shard_map/all_gather | solution.py:121
  390.1 7.4 %collective-permute-start.20 = (f32[1,64,64]{2,1,0:T(8,128)S(1)}, f32[1,64,64]{2,1,0:T(8,128)S(1)}, u32[]{:S(2)}, u32[]{:S(2)}) collective-permute-start(f32[1,64,64]{2,1,0:T(8,128)S(1)} %get-tuple-element.53), channel_id=1, source_target_pairs={{8,0},{16,8},{24,16},{32,24},{40,32},{48,40},{56,48},{64,56},{72,6... | collective-permute-start | bytes 49160 | tf_op jit(solution)/shard_map/ppermute | solution.py:20
  399.5 5.4 collective-permute-done.21
  407.7 2.4 collective-permute-start.23
  410.2 4.9 collective-permute-done.23
  419.3 2.4 collective-permute-start.25
  421.7 4.7 collective-permute-done.25
  426.3 9.9 %collective-permute-start.26 = (f32[6,1,128]{2,1,0:T(1,128)S(1)}, f32[6,1,128]{2,1,0:T(1,128)S(1)}, u32[]{:S(2)}, u32[]{:S(2)}) collective-permute-start(f32[6,1,128]{2,1,0:T(1,128)S(1)} %get-tuple-element.61), channel_id=1, source_target_pairs={{1,0},{2,1},{3,2},{4,3},{5,4},{6,5},{7,6},{9,8},{10,9},{11,10},{12... | collective-permute-start | bytes 9224 | tf_op jit(solution)/shard_map/ppermute | solution.py:20
  438.2 9.6 %collective-permute-done.27 = f32[6,1,128]{2,1,0:T(1,128)S(1)} collective-permute-done((f32[6,1,128]{2,1,0:T(1,128)S(1)}, f32[6,1,128]{2,1,0:T(1,128)S(1)}, u32[]{:S(2)}, u32[]{:S(2)}) %collective-permute-start.27) | collective-permute-done | bytes 3104 | tf_op jit(solution)/shard_map/ppermute | solution.py:17
  449.9 2.4 collective-permute-start.29
  452.4 4.7 collective-permute-done.29
  458.9 3.9 collective-permute-start.31
  462.9 7.6 %collective-permute-done.31 = f32[6,1,128]{2,1,0:T(1,128)S(1)} collective-permute-done((f32[6,1,128]{2,1,0:T(1,128)S(1)}, f32[6,1,128]{2,1,0:T(1,128)S(1)}, u32[]{:S(2)}, u32[]{:S(2)}) %collective-permute-start.31) | collective-permute-done | bytes 3104 | tf_op jit(solution)/shard_map/ppermute | solution.py:17
  476.0 6.0 %collective-permute-start.32 = (f32[1,32,256]{1,0,2:T(1,128)S(1)}, f32[1,32,256]{1,0,2:T(1,128)S(1)}, u32[]{:S(2)}, u32[]{:S(2)}) collective-permute-start(f32[1,32,256]{1,0,2:T(1,128)S(1)} %get-tuple-element.21), channel_id=1, source_target_pairs={{8,0},{16,8},{24,16},{32,24},{40,32},{48,40},{56,48},{64,56},{72,6... | collective-permute-start | bytes 98312 | tf_op jit(solution)/shard_map/ppermute | solution.py:20
  486.5 3.9 collective-permute-start.35
  490.4 7.6 %collective-permute-done.35 = f32[10,1,256]{2,1,0:T(1,128)S(1)} collective-permute-done((f32[10,1,256]{2,1,0:T(1,128)S(1)}, f32[10,1,256]{2,1,0:T(1,128)S(1)}, u32[]{:S(2)}, u32[]{:S(2)}) %collective-permute-start.35) | collective-permute-done | bytes 10272 | tf_op jit(solution)/shard_map/ppermute | solution.py:17
  500.9 2.5 copy.258
  503.4 5.2 fusion.17
  511.5 5.8 collective-permute-start.36
  524.4 3.9 collective-permute-start.39
  528.3 7.6 %collective-permute-done.39 = f32[10,1,256]{2,1,0:T(1,128)S(1)} collective-permute-done((f32[10,1,256]{2,1,0:T(1,128)S(1)}, f32[10,1,256]{2,1,0:T(1,128)S(1)}, u32[]{:S(2)}, u32[]{:S(2)}) %collective-permute-start.39) | collective-permute-done | bytes 10272 | tf_op jit(solution)/shard_map/ppermute | solution.py:17
  537.4 2.3 copy.287
  539.7 2.3 copy.288
  542.8 2.5 copy.265
  545.3 5.3 fusion.24
  553.4 5.8 collective-permute-start.40
  566.2 3.9 collective-permute-start.43
  570.2 7.6 %collective-permute-done.43 = f32[10,1,256]{2,1,0:T(1,128)S(1)} collective-permute-done((f32[10,1,256]{2,1,0:T(1,128)S(1)}, f32[10,1,256]{2,1,0:T(1,128)S(1)}, u32[]{:S(2)}, u32[]{:S(2)}) %collective-permute-start.43) | collective-permute-done | bytes 10272 | tf_op jit(solution)/shard_map/ppermute | solution.py:17
  579.3 2.3 copy.289
  585.4 3.5 copy.272
  588.9 4.9 fusion.28
  (185 shorter events, 123.0 us)
Async XLA Ops:
  3.6 33.0 %copy-start.1 = (f32[8,32,256]{1,0,2:T(8,128)}, f32[8,32,256]{1,0,2:T(8,128)S(1)}, u32[]{:S(2)}) copy-start(f32[8,32,256]{1,0,2:T(8,128)S(1)} %multiply_divide_fusion) | copy-start | bytes 786436
  4.6 8.6 %collective-permute-start.1 = (f32[1,32,256]{1,0,2:T(1,128)}, f32[1,32,256]{1,0,2:T(1,128)S(1)}, u32[]{:S(2)}, u32[]{:S(2)}) collective-permute-start(f32[1,32,256]{1,0,2:T(1,128)} %get-tuple-element.24), channel_id=1, source_target_pairs={{0,8},{8,16},{16,24},{24,32},{32,40},{40,48},{48,56},{56,64},{64,7... | collective-permute-start | bytes 98312 | tf_op jit(solution)/shard_map/ppermute | solution.py:17
  6.5 8.6 %collective-permute-start = (f32[1,32,256]{1,0,2:T(1,128)}, f32[1,32,256]{1,0,2:T(1,128)}, u32[]{:S(2)}, u32[]{:S(2)}) collective-permute-start(f32[1,32,256]{1,0,2:T(1,128)} %get-tuple-element.25), channel_id=1, source_target_pairs={{8,0},{16,8},{24,16},{32,24},{40,32},{48,40},{56,48},{64,56},{72,6... | collective-permute-start | bytes 98312 | tf_op jit(solution)/shard_map/ppermute | solution.py:20
  17.4 5.9 collective-permute-start.2
  21.2 11.6 %collective-permute-start.3 = (f32[10,1,256]{2,1,0:T(1,128)S(1)}, f32[10,1,256]{2,1,0:T(1,128)S(1)}, u32[]{:S(2)}, u32[]{:S(2)}) collective-permute-start(f32[10,1,256]{2,1,0:T(1,128)S(1)} %get-tuple-element.44), channel_id=1, source_target_pairs={{0,1},{1,2},{2,3},{3,4},{4,5},{5,6},{6,7},{8,9},{9,10},{10,11},{11... | collective-permute-start | bytes 30728 | tf_op jit(solution)/shard_map/ppermute | solution.py:17
  32.8 0.6 copy-start.8
  48.3 8.6 %collective-permute-start.5 = (f32[1,32,256]{1,0,2:T(1,128)}, f32[1,32,256]{1,0,2:T(1,128)S(1)}, u32[]{:S(2)}, u32[]{:S(2)}) collective-permute-start(f32[1,32,256]{1,0,2:T(1,128)} %get-tuple-element.22), channel_id=1, source_target_pairs={{0,8},{8,16},{16,24},{24,32},{32,40},{40,48},{48,56},{56,64},{64,7... | collective-permute-start | bytes 98312 | tf_op jit(solution)/shard_map/ppermute | solution.py:17
  50.2 8.6 %collective-permute-start.4 = (f32[1,32,256]{1,0,2:T(1,128)}, f32[1,32,256]{1,0,2:T(1,128)}, u32[]{:S(2)}, u32[]{:S(2)}) collective-permute-start(f32[1,32,256]{1,0,2:T(1,128)} %get-tuple-element.23), channel_id=1, source_target_pairs={{8,0},{16,8},{24,16},{32,24},{40,32},{48,40},{56,48},{64,56},{72,6... | collective-permute-start | bytes 98312 | tf_op jit(solution)/shard_map/ppermute | solution.py:20
  56.9 10.9 %copy-start.4 = (f32[1,32,256]{1,0,2:T(1,128)}, f32[1,32,256]{1,0,2:T(1,128)S(1)}, u32[]{:S(2)}) copy-start(f32[1,32,256]{1,0,2:T(1,128)S(1)} %collective-permute-done.5) | copy-start | bytes 98308
  61.7 31.8 %collective-permute-start.6 = (f32[10,1,256]{2,1,0:T(1,128)}, f32[10,1,256]{2,1,0:T(1,128)S(1)}, u32[]{:S(2)}, u32[]{:S(2)}) collective-permute-start(f32[10,1,256]{2,1,0:T(1,128)} %get-tuple-element.41), channel_id=1, source_target_pairs={{1,0},{2,1},{3,2},{4,3},{5,4},{6,5},{7,6},{9,8},{10,9},{11,10},{12... | collective-permute-start | bytes 30728 | tf_op jit(solution)/shard_map/ppermute | solution.py:20
  63.6 29.9 %collective-permute-start.7 = (f32[10,1,256]{2,1,0:T(1,128)}, f32[10,1,256]{2,1,0:T(1,128)}, u32[]{:S(2)}, u32[]{:S(2)}) collective-permute-start(f32[10,1,256]{2,1,0:T(1,128)} %get-tuple-element.40), channel_id=1, source_target_pairs={{0,1},{1,2},{2,3},{3,4},{4,5},{5,6},{6,7},{8,9},{9,10},{10,11},{11... | collective-permute-start | bytes 30728 | tf_op jit(solution)/shard_map/ppermute | solution.py:17
  86.6 7.0 %copy-start.6 = (f32[1,32,256]{2,1,0:T(8,128)S(1)}, f32[1,32,256]{2,1,0:T(8,128)}, u32[]{:S(2)}) copy-start(f32[1,32,256]{2,1,0:T(8,128)} %copy.231) | copy-start | bytes 98308
  86.6 7.0 %copy-start.7 = (f32[1,32,256]{2,1,0:T(8,128)S(1)}, f32[1,32,256]{2,1,0:T(8,128)}, u32[]{:S(2)}) copy-start(f32[1,32,256]{2,1,0:T(8,128)} %copy.233) | copy-start | bytes 98308
  101.2 3.5 copy-start.5
  136.3 7.3 %collective-permute-start.8 = (f32[1,16,128]{2,1,0:T(8,128)S(1)}, f32[1,16,128]{2,1,0:T(8,128)S(1)}, u32[]{:S(2)}, u32[]{:S(2)}) collective-permute-start(f32[1,16,128]{2,1,0:T(8,128)S(1)} %get-tuple-element.75), channel_id=1, source_target_pairs={{8,0},{16,8},{24,16},{32,24},{40,32},{48,40},{56,48},{64,56},{72,6... | collective-permute-start | bytes 24584 | tf_op jit(solution)/shard_map/ppermute | solution.py:20
  141.6 7.1 %collective-permute-start.9 = (f32[1,16,128]{2,1,0:T(8,128)S(1)}, f32[1,16,128]{2,1,0:T(8,128)S(1)}, u32[]{:S(2)}, u32[]{:S(2)}) collective-permute-start(f32[1,16,128]{2,1,0:T(8,128)S(1)} %get-tuple-element.74), channel_id=1, source_target_pairs={{0,8},{8,16},{16,24},{24,32},{32,40},{40,48},{48,56},{56,64},{64,7... | collective-permute-start | bytes 24584 | tf_op jit(solution)/shard_map/ppermute | solution.py:17
  148.7 15.4 %collective-permute-start.10 = (f32[6,1,128]{2,1,0:T(1,128)S(1)}, f32[6,1,128]{2,1,0:T(1,128)S(1)}, u32[]{:S(2)}, u32[]{:S(2)}) collective-permute-start(f32[6,1,128]{2,1,0:T(1,128)S(1)} %get-tuple-element.65), channel_id=1, source_target_pairs={{1,0},{2,1},{3,2},{4,3},{5,4},{6,5},{7,6},{9,8},{10,9},{11,10},{12... | collective-permute-start | bytes 9224 | tf_op jit(solution)/shard_map/ppermute | solution.py:20
  156.9 11.5 %collective-permute-start.11 = (f32[6,1,128]{2,1,0:T(1,128)S(1)}, f32[6,1,128]{2,1,0:T(1,128)S(1)}, u32[]{:S(2)}, u32[]{:S(2)}) collective-permute-start(f32[6,1,128]{2,1,0:T(1,128)S(1)} %get-tuple-element.64), channel_id=1, source_target_pairs={{0,1},{1,2},{2,3},{3,4},{4,5},{5,6},{6,7},{8,9},{9,10},{10,11},{11... | collective-permute-start | bytes 9224 | tf_op jit(solution)/shard_map/ppermute | solution.py:17
  168.7 4.4 collective-permute-start.12
  170.6 7.1 %collective-permute-start.13 = (f32[1,16,128]{2,1,0:T(8,128)S(1)}, f32[1,16,128]{2,1,0:T(8,128)S(1)}, u32[]{:S(2)}, u32[]{:S(2)}) collective-permute-start(f32[1,16,128]{2,1,0:T(8,128)S(1)} %get-tuple-element.72), channel_id=1, source_target_pairs={{0,8},{8,16},{16,24},{24,32},{32,40},{40,48},{48,56},{56,64},{64,7... | collective-permute-start | bytes 24584 | tf_op jit(solution)/shard_map/ppermute | solution.py:17
  177.7 51.3 %collective-permute-start.14 = (f32[6,1,128]{2,1,0:T(1,128)S(1)}, f32[6,1,128]{2,1,0:T(1,128)S(1)}, u32[]{:S(2)}, u32[]{:S(2)}) collective-permute-start(f32[6,1,128]{2,1,0:T(1,128)S(1)} %get-tuple-element.63), channel_id=1, source_target_pairs={{1,0},{2,1},{3,2},{4,3},{5,4},{6,5},{7,6},{9,8},{10,9},{11,10},{12... | collective-permute-start | bytes 9224 | tf_op jit(solution)/shard_map/ppermute | solution.py:20
  183.3 45.7 %collective-permute-start.15 = (f32[6,1,128]{2,1,0:T(1,128)S(1)}, f32[6,1,128]{2,1,0:T(1,128)S(1)}, u32[]{:S(2)}, u32[]{:S(2)}) collective-permute-start(f32[6,1,128]{2,1,0:T(1,128)S(1)} %get-tuple-element.62), channel_id=1, source_target_pairs={{0,1},{1,2},{2,3},{3,4},{4,5},{5,6},{6,7},{8,9},{9,10},{10,11},{11... | collective-permute-start | bytes 9224 | tf_op jit(solution)/shard_map/ppermute | solution.py:17
  278.4 4.6 collective-permute-start.16
  280.5 7.3 %collective-permute-start.17 = (f32[1,64,64]{2,1,0:T(8,128)S(1)}, f32[1,64,64]{2,1,0:T(8,128)S(1)}, u32[]{:S(2)}, u32[]{:S(2)}) collective-permute-start(f32[1,64,64]{2,1,0:T(8,128)S(1)} %get-tuple-element.56), channel_id=1, source_target_pairs={{0,8},{8,16},{16,24},{24,32},{32,40},{40,48},{48,56},{56,64},{64,7... | collective-permute-start | bytes 49160 | tf_op jit(solution)/shard_map/ppermute | solution.py:17
  288.7 4.4 collective-permute-start.18
  290.6 7.3 %collective-permute-start.19 = (f32[1,64,64]{2,1,0:T(8,128)S(1)}, f32[1,64,64]{2,1,0:T(8,128)S(1)}, u32[]{:S(2)}, u32[]{:S(2)}) collective-permute-start(f32[1,64,64]{2,1,0:T(8,128)S(1)} %get-tuple-element.54), channel_id=1, source_target_pairs={{0,8},{8,16},{16,24},{24,32},{32,40},{40,48},{48,56},{56,64},{64,7... | collective-permute-start | bytes 49160 | tf_op jit(solution)/shard_map/ppermute | solution.py:17
  390.1 9.4 %collective-permute-start.20 = (f32[1,64,64]{2,1,0:T(8,128)S(1)}, f32[1,64,64]{2,1,0:T(8,128)S(1)}, u32[]{:S(2)}, u32[]{:S(2)}) collective-permute-start(f32[1,64,64]{2,1,0:T(8,128)S(1)} %get-tuple-element.53), channel_id=1, source_target_pairs={{8,0},{16,8},{24,16},{32,24},{40,32},{48,40},{56,48},{64,56},{72,6... | collective-permute-start | bytes 49160 | tf_op jit(solution)/shard_map/ppermute | solution.py:20
  397.6 7.3 %collective-permute-start.21 = (f32[1,64,64]{2,1,0:T(8,128)S(1)}, f32[1,64,64]{2,1,0:T(8,128)S(1)}, u32[]{:S(2)}, u32[]{:S(2)}) collective-permute-start(f32[1,64,64]{2,1,0:T(8,128)S(1)} %get-tuple-element.52), channel_id=1, source_target_pairs={{0,8},{8,16},{16,24},{24,32},{32,40},{40,48},{48,56},{56,64},{64,7... | collective-permute-start | bytes 49160 | tf_op jit(solution)/shard_map/ppermute | solution.py:17
  405.8 4.3 collective-permute-start.22
  407.7 7.3 %collective-permute-start.23 = (f32[1,64,64]{2,1,0:T(8,128)S(1)}, f32[1,64,64]{2,1,0:T(8,128)S(1)}, u32[]{:S(2)}, u32[]{:S(2)}) collective-permute-start(f32[1,64,64]{2,1,0:T(8,128)S(1)} %get-tuple-element.50), channel_id=1, source_target_pairs={{0,8},{8,16},{16,24},{24,32},{32,40},{40,48},{48,56},{56,64},{64,7... | collective-permute-start | bytes 49160 | tf_op jit(solution)/shard_map/ppermute | solution.py:17
  417.3 4.3 collective-permute-start.24
  419.3 7.1 %collective-permute-start.25 = (f32[1,16,128]{2,1,0:T(8,128)S(1)}, f32[1,16,128]{2,1,0:T(8,128)S(1)}, u32[]{:S(2)}, u32[]{:S(2)}) collective-permute-start(f32[1,16,128]{2,1,0:T(8,128)S(1)} %get-tuple-element.68), channel_id=1, source_target_pairs={{0,8},{8,16},{16,24},{24,32},{32,40},{40,48},{48,56},{56,64},{64,7... | collective-permute-start | bytes 24584 | tf_op jit(solution)/shard_map/ppermute | solution.py:17
  426.3 11.9 %collective-permute-start.26 = (f32[6,1,128]{2,1,0:T(1,128)S(1)}, f32[6,1,128]{2,1,0:T(1,128)S(1)}, u32[]{:S(2)}, u32[]{:S(2)}) collective-permute-start(f32[6,1,128]{2,1,0:T(1,128)S(1)} %get-tuple-element.61), channel_id=1, source_target_pairs={{1,0},{2,1},{3,2},{4,3},{5,4},{6,5},{7,6},{9,8},{10,9},{11,10},{12... | collective-permute-start | bytes 9224 | tf_op jit(solution)/shard_map/ppermute | solution.py:20
  436.3 11.5 %collective-permute-start.27 = (f32[6,1,128]{2,1,0:T(1,128)S(1)}, f32[6,1,128]{2,1,0:T(1,128)S(1)}, u32[]{:S(2)}, u32[]{:S(2)}) collective-permute-start(f32[6,1,128]{2,1,0:T(1,128)S(1)} %get-tuple-element.60), channel_id=1, source_target_pairs={{0,1},{1,2},{2,3},{3,4},{4,5},{5,6},{6,7},{8,9},{9,10},{10,11},{11... | collective-permute-start | bytes 9224 | tf_op jit(solution)/shard_map/ppermute | solution.py:17
  448.0 4.3 collective-permute-start.28
  449.9 7.1 %collective-permute-start.29 = (f32[1,16,128]{2,1,0:T(8,128)S(1)}, f32[1,16,128]{2,1,0:T(8,128)S(1)}, u32[]{:S(2)}, u32[]{:S(2)}) collective-permute-start(f32[1,16,128]{2,1,0:T(8,128)S(1)} %get-tuple-element.66), channel_id=1, source_target_pairs={{0,8},{8,16},{16,24},{24,32},{32,40},{40,48},{48,56},{56,64},{64,7... | collective-permute-start | bytes 24584 | tf_op jit(solution)/shard_map/ppermute | solution.py:17
  457.0 5.8 collective-permute-start.30
  458.9 11.5 %collective-permute-start.31 = (f32[6,1,128]{2,1,0:T(1,128)S(1)}, f32[6,1,128]{2,1,0:T(1,128)S(1)}, u32[]{:S(2)}, u32[]{:S(2)}) collective-permute-start(f32[6,1,128]{2,1,0:T(1,128)S(1)} %get-tuple-element.58), channel_id=1, source_target_pairs={{0,1},{1,2},{2,3},{3,4},{4,5},{5,6},{6,7},{8,9},{9,10},{10,11},{11... | collective-permute-start | bytes 9224 | tf_op jit(solution)/shard_map/ppermute | solution.py:17
  472.9 1.0 copy-start.2
  474.1 9.5 %collective-permute-start.33 = (f32[1,32,256]{1,0,2:T(1,128)S(1)}, f32[1,32,256]{1,0,2:T(1,128)S(1)}, u32[]{:S(2)}, u32[]{:S(2)}) collective-permute-start(f32[1,32,256]{1,0,2:T(1,128)S(1)} %get-tuple-element.20), channel_id=1, source_target_pairs={{0,8},{8,16},{16,24},{24,32},{32,40},{40,48},{48,56},{56,64},{64,7... | collective-permute-start | bytes 98312 | tf_op jit(solution)/shard_map/ppermute | solution.py:17
  476.0 8.4 %collective-permute-start.32 = (f32[1,32,256]{1,0,2:T(1,128)S(1)}, f32[1,32,256]{1,0,2:T(1,128)S(1)}, u32[]{:S(2)}, u32[]{:S(2)}) collective-permute-start(f32[1,32,256]{1,0,2:T(1,128)S(1)} %get-tuple-element.21), channel_id=1, source_target_pairs={{8,0},{16,8},{24,16},{32,24},{40,32},{48,40},{56,48},{64,56},{72,6... | collective-permute-start | bytes 98312 | tf_op jit(solution)/shard_map/ppermute | solution.py:20
  484.5 5.9 collective-permute-start.34
  486.5 11.6 %collective-permute-start.35 = (f32[10,1,256]{2,1,0:T(1,128)S(1)}, f32[10,1,256]{2,1,0:T(1,128)S(1)}, u32[]{:S(2)}, u32[]{:S(2)}) collective-permute-start(f32[10,1,256]{2,1,0:T(1,128)S(1)} %get-tuple-element.36), channel_id=1, source_target_pairs={{0,1},{1,2},{2,3},{3,4},{4,5},{5,6},{6,7},{8,9},{9,10},{10,11},{11... | collective-permute-start | bytes 30728 | tf_op jit(solution)/shard_map/ppermute | solution.py:17
  508.6 31.2 %copy-start = (f32[8,32,256]{1,0,2:T(8,128)}, f32[8,32,256]{1,0,2:T(8,128)S(1)}, u32[]{:S(2)}) copy-start(f32[8,32,256]{1,0,2:T(8,128)S(1)} %fusion.17) | copy-start | bytes 786436
  509.6 8.6 %collective-permute-start.37 = (f32[1,32,256]{1,0,2:T(1,128)}, f32[1,32,256]{1,0,2:T(1,128)S(1)}, u32[]{:S(2)}, u32[]{:S(2)}) collective-permute-start(f32[1,32,256]{1,0,2:T(1,128)} %get-tuple-element.18), channel_id=1, source_target_pairs={{0,8},{8,16},{16,24},{24,32},{32,40},{40,48},{48,56},{56,64},{64,7... | collective-permute-start | bytes 98312 | tf_op jit(solution)/shard_map/ppermute | solution.py:17
  511.5 8.6 %collective-permute-start.36 = (f32[1,32,256]{1,0,2:T(1,128)}, f32[1,32,256]{1,0,2:T(1,128)}, u32[]{:S(2)}, u32[]{:S(2)}) collective-permute-start(f32[1,32,256]{1,0,2:T(1,128)} %get-tuple-element.19), channel_id=1, source_target_pairs={{8,0},{16,8},{24,16},{32,24},{40,32},{48,40},{56,48},{64,56},{72,6... | collective-permute-start | bytes 98312 | tf_op jit(solution)/shard_map/ppermute | solution.py:20
  522.5 5.9 collective-permute-start.38
  524.4 11.6 %collective-permute-start.39 = (f32[10,1,256]{2,1,0:T(1,128)S(1)}, f32[10,1,256]{2,1,0:T(1,128)S(1)}, u32[]{:S(2)}, u32[]{:S(2)}) collective-permute-start(f32[10,1,256]{2,1,0:T(1,128)S(1)} %get-tuple-element.32), channel_id=1, source_target_pairs={{0,1},{1,2},{2,3},{3,4},{4,5},{5,6},{6,7},{8,9},{9,10},{10,11},{11... | collective-permute-start | bytes 30728 | tf_op jit(solution)/shard_map/ppermute | solution.py:17
  536.0 0.6 copy-start.9
  551.5 8.6 %collective-permute-start.41 = (f32[1,32,256]{1,0,2:T(1,128)}, f32[1,32,256]{1,0,2:T(1,128)S(1)}, u32[]{:S(2)}, u32[]{:S(2)}) collective-permute-start(f32[1,32,256]{1,0,2:T(1,128)} %get-tuple-element.16), channel_id=1, source_target_pairs={{0,8},{8,16},{16,24},{24,32},{32,40},{40,48},{48,56},{56,64},{64,7... | collective-permute-start | bytes 98312 | tf_op jit(solution)/shard_map/ppermute | solution.py:17
  553.4 8.6 %collective-permute-start.40 = (f32[1,32,256]{1,0,2:T(1,128)}, f32[1,32,256]{1,0,2:T(1,128)}, u32[]{:S(2)}, u32[]{:S(2)}) collective-permute-start(f32[1,32,256]{1,0,2:T(1,128)} %get-tuple-element.17), channel_id=1, source_target_pairs={{8,0},{16,8},{24,16},{32,24},{40,32},{48,40},{56,48},{64,56},{72,6... | collective-permute-start | bytes 98312 | tf_op jit(solution)/shard_map/ppermute | solution.py:20
  559.5 25.9 %copy-start.3 = (f32[8,32,256]{2,1,0:T(8,128)}, f32[8,32,256]{2,1,0:T(8,128)S(1)}, u32[]{:S(2)}) copy-start(f32[8,32,256]{2,1,0:T(8,128)S(1)} %copy.274) | copy-start | bytes 786436
  564.3 5.9 collective-permute-start.42
  566.2 11.6 %collective-permute-start.43 = (f32[10,1,256]{2,1,0:T(1,128)S(1)}, f32[10,1,256]{2,1,0:T(1,128)S(1)}, u32[]{:S(2)}, u32[]{:S(2)}) collective-permute-start(f32[10,1,256]{2,1,0:T(1,128)S(1)} %get-tuple-element.28), channel_id=1, source_target_pairs={{0,1},{1,2},{2,3},{3,4},{4,5},{5,6},{6,7},{8,9},{9,10},{10,11},{11... | collective-permute-start | bytes 30728 | tf_op jit(solution)/shard_map/ppermute | solution.py:17
  577.8 0.6 copy-start.10
where the time goes:
time: 604 us; the launch traced here: 597 us
  blocking collectives  160 us (26%)
  starting transfers between devices  146 us (24%)
  local copies, waits for them, and re-layouts  114 us (19%)
  waiting for transfers between devices  101 us (17%)
  other arithmetic  64.5 us (11%)
  matrix products  8.31 us (1%)
    ppermute x22, waiting for transfers between devices, padded_2(): lax.ppermute(lax.slice_in_dim(block, block.shape[dim] - width, None, axis...  95.2 us
    ppermute x22, starting transfers between devices, padded_2(): lax.ppermute(lax.slice_in_dim(block, 0, width, axis=dim), axis, backward)  90.6 us
    ppermute x22, starting transfers between devices, padded_2(): lax.ppermute(lax.slice_in_dim(block, block.shape[dim] - width, None, axis...  55.5 us
    all_gather x1, blocking collectives, per_device(): lax.all_gather(screens[2], 'narrow', axis=1, tiled=True)  43.8 us
    all_gather x1, blocking collectives, per_device(): lax.all_gather(sources[2], 'narrow', axis=1, tiled=True)  43.8 us
    all_gather x1, blocking collectives, per_device(): lax.all_gather(part_screen, 'wide', axis=0, tiled=True)  40.5 us
    reshape x3, local copies, waits for them, and re-layouts, coarsen(): values.reshape(extent[0] // 2, 2, extent[1] // 2, 2, extent[2] // 2, 2)  40.3 us
    all_gather x1, blocking collectives, per_device(): lax.all_gather(part_source, 'wide', axis=0, tiled=True)  31.8 us
  transfers between devices with their start and end apart: 44, of which 24 were waited for; matrix products, arithmetic and copies ran while one was open for 6% of the time, Pallas kernels for 0%

commit v1 on v0

v1 whole, which is shorter than its diff:
```python
import functools

import numpy as np
import jax
import jax.numpy as jnp
from jax import lax
from jax.experimental import pallas as pl
from jax.experimental.pallas import tpu as pltpu
from jax.sharding import PartitionSpec as P

MESH = pl.DeviceIdType.MESH
F32 = jnp.float32
OMEGA = 0.8
KEEP = 0.2
WINDOW = 24


def sine_table(count):
    ladder = np.arange(count, dtype=np.float64) + 1.0
    return np.sin(np.pi * ladder[:, None] * ladder[None, :] / (count + 1.0))


def sine_eigen(count):
    ladder = np.arange(count, dtype=np.float64) + 1.0
    return 2.0 - 2.0 * np.cos(np.pi * ladder / (count + 1.0))


def tables(wide, narrow):
    count_y, count_z = 4 * narrow, 32
    sine_x, sine_y, sine_z = sine_table(wide), sine_table(count_y), sine_table(count_z)
    to_modes = np.tile(np.repeat(sine_z.T, 2, axis=0), (2, 4))
    from_modes = np.tile(np.repeat(sine_z, 2, axis=1), (4, 2))
    rows_y = 0.5 * np.repeat(sine_y, 2, axis=1)
    rows_y = np.pad(rows_y, ((0, 0), (0, 128 - rows_y.shape[1])))
    eigen_y = sine_eigen(count_y).reshape(4, narrow)
    eigen = eigen_y.T[:, :, None] + sine_eigen(count_z)[None, None, :]
    eigen = eigen.reshape(narrow, 128)
    common = np.concatenate([to_modes, from_modes, rows_y, eigen], axis=0)
    inverse_x = np.pad(sine_x, ((2, 2), (0, 0)))
    inverse_x = np.repeat(inverse_x[:, :, None], 128, axis=2)
    fine_y = np.pad(np.repeat(sine_y, 2, axis=0), ((8, 8), (0, 0)))
    inverse_y = np.zeros((narrow, 4, WINDOW, 128))
    for n in range(narrow):
        for g in range(4):
            inverse_y[n, g, :, :narrow] = fine_y[8 * n : 8 * n + WINDOW, g * narrow : (g + 1) * narrow]
    inverse_y = inverse_y.reshape(narrow, 4 * WINDOW, 128)
    return [a.astype(np.float32) for a in (common, inverse_x, inverse_y)]


def rolled(value, shift, axis):
    return pltpu.roll(value, shift % value.shape[axis], axis)


def lanes_of(rows):
    return lax.broadcasted_iota(jnp.int32, (rows, 128), 1)


def z_sum_halves(low, high):
    lane = lanes_of(low.shape[0])
    up_low, up_high = rolled(low, -1, 1), rolled(high, -1, 1)
    down_low, down_high = rolled(low, 1, 1), rolled(high, 1, 1)
    last, first = lane == 127, lane == 0
    sum_low = jnp.where(last, up_high, up_low) + jnp.where(first, 0.0, down_low)
    sum_high = jnp.where(last, 0.0, up_high) + jnp.where(first, down_low, down_high)
    return sum_low, sum_high


def z_sum(value, period):
    lane = lanes_of(value.shape[0]) % period
    up = jnp.where(lane == period - 1, 0.0, rolled(value, -1, 1))
    return up + jnp.where(lane == 0, 0.0, rolled(value, 1, 1))


def fine_sum(ref, r, a, n):
    centre = [ref[r, h, pl.ds(a, n), :] for h in range(2)]
    along_z = z_sum_halves(*centre)
    summed = []
    for h in range(2):
        along_x = ref[r - 1, h, pl.ds(a, n), :] + ref[r + 1, h, pl.ds(a, n), :]
        along_y = ref[r, h, pl.ds(a - 1, n), :] + ref[r, h, pl.ds(a + 1, n), :]
        summed.append(along_x + along_y + along_z[h])
    return centre, summed


def middle_sum(ref, r, a, n):
    centre = ref[r, pl.ds(a, n), :]
    along_x = ref[r - 1, pl.ds(a, n), :] + ref[r + 1, pl.ds(a, n), :]
    along_y = ref[r, pl.ds(a - 1, n), :] + ref[r, pl.ds(a + 1, n), :]
    return centre, along_x + along_y + z_sum(centre, 128)


def pair_x_sum(before, here, after):
    return here + jnp.where(lanes_of(here.shape[0]) < 64, before, after)


def fold_lanes(low, high):
    rows = low.shape[0]
    lane = lanes_of(rows)
    index = (lane * 2) % 128
    low = jnp.take_along_axis(low + rolled(low, -1, 1), index, axis=1)
    high = jnp.take_along_axis(high + rolled(high, -1, 1), index, axis=1)
    return jnp.where(lane < 64, low, high)


def spread_lanes(value):
    lane = lanes_of(value.shape[0])
    index = lane // 2
    return jnp.take_along_axis(value, index, axis=1), jnp.take_along_axis(value, index + 64, axis=1)


def dot(a, b):
    return jnp.dot(a, b, precision=lax.Precision.HIGHEST, preferred_element_type=F32)


def cycle_kernel(
    W, N,
    f_hbm, s_hbm, common_hbm, invx_hbm, invy_hbm,
    out_hbm, res_hbm,
    f_in, s_in, common, invx, invy, out_v, res_v,
    va, wa, v2a, ua, ub, fold,
    vb, wb, v2b, tb, ub1, ub2, fb, db, foldb,
    gvw, gv2, t2, u2,
    modes,
    in_sem, out_sem, send_sem, recv_sem, gather_send, gather_recv, wide_send, wide_recv,
):
    i = lax.axis_index("wide")
    n = lax.axis_index("narrow")

    loads = [
        pltpu.make_async_copy(src, dst, in_sem.at[k])
        for k, (src, dst) in enumerate(
            (
                (s_hbm, s_in),
                (f_hbm, f_in),
                (common_hbm, common),
                (invx_hbm.at[pl.ds(i, 5)], invx),
                (invy_hbm.at[n], invy),
            )
        )
    ]
    for load in loads:
        load.start()

    barrier = pltpu.get_barrier_semaphore()

    def greet(wide_id, narrow_id):
        pl.semaphore_signal(barrier, inc=1, device_id=(wide_id, narrow_id), device_id_type=MESH)

    has_low, has_high = i > 0, i < W - 1

    def greet_narrow(k, _):
        other = lax.rem(n + k, N)
        greet(i, other)

        @pl.when(has_low)
        def _():
            greet(i - 1, other)

        @pl.when(has_high)
        def _():
            greet(i + 1, other)

        return 0

    lax.fori_loop(1, N, greet_narrow, 0)

    def greet_wide(k, _):
        greet(lax.rem(i + k, W), n)
        return 0

    lax.fori_loop(1, W, greet_wide, 0)

    def zero(ref, *index):
        shape = ref.at[index].shape if index else ref.shape
        ref[index if index else ...] = jnp.zeros(shape, F32)

    all_ = slice(None)

    @pl.when(i == 0)
    def _():
        for ref in (va, wa):
            zero(ref, pl.ds(0, 4))
        for ref in (vb, wb, v2b):
            zero(ref, pl.ds(0, 4))
        zero(gvw, pl.ds(0, 2))
        zero(gv2, pl.ds(0, 2))

    @pl.when(i == W - 1)
    def _():
        for ref in (va, wa):
            zero(ref, pl.ds(12, 4))
        for ref in (vb, wb, v2b):
            zero(ref, pl.ds(8, 4))
        zero(gvw, pl.ds(3, 2))
        zero(gv2, pl.ds(3, 2))

    @pl.when(i == 1)
    def _():
        zero(gvw, 0)
        zero(gv2, 0)

    @pl.when(i == W - 2)
    def _():
        zero(gvw, 4)
        zero(gv2, 4)

    @pl.when(n == 0)
    def _():
        for ref in (va, wa):
            zero(ref, all_, all_, pl.ds(0, 8))
        for ref in (vb, wb, v2b):
            zero(ref, all_, pl.ds(0, 8))

    @pl.when(n == N - 1)
    def _():
        for ref in (va, wa):
            zero(ref, all_, all_, pl.ds(40, 8))
        for ref in (vb, wb, v2b):
            zero(ref, all_, pl.ds(24, 8))

    cols = 8 * N
    zero(gvw, pl.ds(1, 3), all_, pl.ds(0, 8))
    zero(gvw, pl.ds(1, 3), all_, pl.ds(8 + cols, 8))
    zero(gv2, 2, pl.ds(0, 8))
    zero(gv2, 2, pl.ds(8 + cols, 8))
    zero(t2, all_, pl.ds(0, 8))
    zero(t2, all_, pl.ds(8 + cols, 8))

    loads[0].wait()
    loads[1].wait()

    def start_fine(r, _):
        for h in range(2):
            screen = s_in[r, :, pl.ds(128 * h, 128)]
            weight = OMEGA / (6.0 + screen)
            wa[r + 4, h, pl.ds(8, 32), :] = weight
            va[r + 4, h, pl.ds(8, 32), :] = f_in[r, :, pl.ds(128 * h, 128)] * weight
        return 0

    lax.fori_loop(0, 8, start_fine, 0)

    counter = [0]

    def span(step, first, size, depths):
        if step == 0:
            return pl.ds(first, size), pl.ds(first, size)
        low, high = depths
        count = high - low + 1
        if step > 0:
            return pl.ds(first + size - high, count), pl.ds(first - high, count)
        return pl.ds(first + low - 1, count), pl.ds(first + size + low - 1, count)

    def there(dx, dy):
        terms = []
        if dx > 0:
            terms.append(i < W - dx)
        if dx < 0:
            terms.append(i >= -dx)
        if dy > 0:
            terms.append(n < N - dy)
        if dy < 0:
            terms.append(n >= -dy)
        return functools.reduce(jnp.logical_and, terms)

    def exchange(src, dst, dx, dy):
        k = counter[0]
        counter[0] += 1
        copy = pltpu.make_async_remote_copy(
            src_ref=src, dst_ref=dst, send_sem=send_sem.at[k], recv_sem=recv_sem.at[k],
            device_id=(lax.rem(i + dx + W, W), lax.rem(n + dy + N, N)), device_id_type=MESH,
        )
        return copy, there(dx, dy), there(-dx, -dy)

    def fine_piece(ref, dx, dy, depth_x=None, depth_y=None):
        src_x, dst_x = span(dx, 4, 8, depth_x)
        src_y, dst_y = span(dy, 8, 32, depth_y)
        return exchange(ref.at[src_x, :, src_y, :], ref.at[dst_x, :, dst_y, :], dx, dy)

    def middle_piece(ref, dx, dy, depth_x=None, depth_y=None):
        src_x, dst_x = span(dx, 4, 4, depth_x)
        src_y, dst_y = span(dy, 8, 16, depth_y)
        return exchange(ref.at[src_x, src_y, :], ref.at[dst_x, dst_y, :], dx, dy)

    sides = (-1, 1)
    corners = [(dx, dy) for dx in sides for dy in sides]

    def start(pieces):
        for copy, to, _ in pieces:
            pl.when(to)(copy.start)

    def receive(pieces):
        for copy, _, come in pieces:
            pl.when(come)(copy.wait_recv)

    def sent(pieces):
        for copy, to, _ in pieces:
            pl.when(to)(copy.wait_send)

    fine_near = (
        [fine_piece(va, 0, d, None, (1, 2)) for d in sides]
        + [fine_piece(wa, 0, d, None, (1, 1)) for d in sides]
        + [fine_piece(va, dx, dy, (1, 1), (1, 1)) for dx, dy in corners]
        + [fine_piece(va, d, 0, (1, 2)) for d in sides]
        + [fine_piece(wa, d, 0, (1, 1)) for d in sides]
    )
    fine_far = (
        [fine_piece(va, 0, d, None, (3, 4)) for d in sides]
        + [fine_piece(wa, 0, d, None, (2, 3)) for d in sides]
        + [fine_piece(va, dx, dy, (1, 1), (2, 3)) for dx, dy in corners]
        + [fine_piece(va, dx, dy, (2, 3), (1, 2)) for dx, dy in corners]
        + [fine_piece(wa, dx, dy, (1, 2), (1, 2)) for dx, dy in corners]
        + [fine_piece(va, d, 0, (3, 4)) for d in sides]
        + [fine_piece(wa, d, 0, (2, 3)) for d in sides]
    )

    def middle_pieces(ref, depth, corner):
        return (
            [middle_piece(ref, 0, d, None, (1, depth)) for d in sides]
            + [middle_piece(ref, dx, dy, (1, corner), (1, corner)) for dx, dy in corners]
            + [middle_piece(ref, d, 0, (1, depth)) for d in sides]
        )

    middle_w = middle_pieces(wb, 3, 2)
    middle_v = middle_pieces(vb, 3, 2)
    middle_v2 = middle_pieces(v2b, 4, 3)

    window = pl.ds(pl.multiple_of(8 * n, 8), WINDOW)
    coarse_far = [exchange(gv2.at[2, window, :], gv2.at[2 - d, window, :], d, 0) for d in (-1, 1, -2, 2)]
    coarse_far += [exchange(gvw.at[2, :, window, :], gvw.at[2 - d, :, window, :], d, 0) for d in (-2, 2)]

    greeted = (W - 1) + (N - 1) * (1 + has_low.astype(jnp.int32) + has_high.astype(jnp.int32))
    pl.semaphore_wait(barrier, greeted)

    start(fine_near)
    start(fine_far)

    def screen_middle(q, _):
        for h in range(2):
            lanes = pl.ds(128 * h, 128)
            fold[q, h, :, :] = s_in[2 * q, :, lanes] + s_in[2 * q + 1, :, lanes]
        low, high = (
            fold[q, h, pl.ds(0, 16, stride=2), :] + fold[q, h, pl.ds(1, 16, stride=2), :] for h in range(2)
        )
        diagonal = 6.0 + 0.125 * fold_lanes(low, high)
        db[q, :, :] = diagonal
        wb[q + 4, pl.ds(8, 16), :] = OMEGA / diagonal
        return 0

    lax.fori_loop(0, 4, screen_middle, 0)
    start(middle_w)

    for h in range(2):
        foldb[h, :, :] = (db[2 * h, :, :] - 6.0) + (db[2 * h + 1, :, :] - 6.0)
    low, high = (foldb[h, pl.ds(0, 8, stride=2), :] + foldb[h, pl.ds(1, 8, stride=2), :] for h in range(2))
    coarse_d = 6.0 + 0.125 * fold_lanes(low, high)
    own_cols = pl.ds(pl.multiple_of(8 + 8 * n, 8), 8)
    gvw[2, 1, own_cols, :] = coarse_d

    def fine_v2(a, count, r, _):
        centre, summed = fine_sum(va, r, a, count)
        for h in range(2):
            v2a[r, h, pl.ds(a, count), :] = (1.0 + KEEP) * centre[h] + wa[r, h, pl.ds(a, count), :] * summed[h]
        return 0

    receive(fine_near)
    fine_v2(8, 32, 3, 0)
    lax.fori_loop(4, 12, functools.partial(fine_v2, 7, 34), 0)
    fine_v2(8, 32, 12, 0)

    def fine_residual(ref, r, h, centre, summed):
        lanes = pl.ds(128 * h, 128)
        return f_in[r, :, lanes] - (6.0 + s_in[r, :, lanes]) * centre + summed

    def fine_down(q, _):
        c0, n0 = fine_sum(v2a, 2 * q + 4, 8, 32)
        c1, n1 = fine_sum(v2a, 2 * q + 5, 8, 32)
        for h in range(2):
            fold[q, h, :, :] = fine_residual(v2a, 2 * q, h, c0[h], n0[h]) + fine_residual(
                v2a, 2 * q + 1, h, c1[h], n1[h]
            )
        low, high = (
            fold[q, h, pl.ds(0, 16, stride=2), :] + fold[q, h, pl.ds(1, 16, stride=2), :] for h in range(2)
        )
        source = 0.5 * fold_lanes(low, high)
        fb[q, :, :] = source
        vb[q + 4, pl.ds(8, 16), :] = source * wb[q + 4, pl.ds(8, 16), :]
        return 0

    lax.fori_loop(0, 4, fine_down, 0)
    start(middle_v)

    receive(fine_far)
    lax.fori_loop(1, 15, functools.partial(fine_v2, 4, 40), 0)

    receive(middle_w)
    receive(middle_v)
    for r in range(3, 9):
        centre, summed = middle_sum(vb, r, 4, 24)
        tb[r, pl.ds(4, 24), :] = (1.0 + KEEP) * centre + wb[r, pl.ds(4, 24), :] * summed
    for r in range(4):
        centre, summed = middle_sum(tb, r + 4, 8, 16)
        v2b[r + 4, pl.ds(8, 16), :] = centre
        rest = fb[r, :, :] - db[r, :, :] * centre + summed
        if r % 2 == 0:
            held = rest
        else:
            foldb[r // 2, :, :] = held + rest
    low, high = (foldb[h, pl.ds(0, 8, stride=2), :] + foldb[h, pl.ds(1, 8, stride=2), :] for h in range(2))
    gvw[2, 0, own_cols, :] = 0.5 * fold_lanes(low, high) * (OMEGA / coarse_d)

    def gather_copy(dx, k):
        other = lax.rem(n + k, N)
        target = lax.rem(i + dx + W, W)
        return pltpu.make_async_remote_copy(
            src_ref=gvw.at[2, :, own_cols, :], dst_ref=gvw.at[2 - dx, :, own_cols, :],
            send_sem=gather_send.at[dx + 1, k], recv_sem=gather_recv.at[1 - dx, n],
            device_id=(target, other), device_id_type=MESH,
        )

    def arrived(slot, k):
        other = lax.rem(n + k, N)
        cells = pl.ds(pl.multiple_of(8 + 8 * other, 8), 8)
        return pltpu.make_async_remote_copy(
            src_ref=gvw.at[2, :, own_cols, :], dst_ref=gvw.at[1 + slot, :, cells, :],
            send_sem=gather_send.at[0, 0], recv_sem=gather_recv.at[slot, other],
            device_id=(lax.rem(i + 1, W), n), device_id_type=MESH,
        )

    def gather_start(k, _):
        @pl.when(k > 0)
        def _():
            gather_copy(0, k).start()

        @pl.when(has_low)
        def _():
            gather_copy(-1, k).start()

        @pl.when(has_high)
        def _():
            gather_copy(1, k).start()

        return 0

    def gather_receive(k, _):
        @pl.when(k > 0)
        def _():
            arrived(1, k).wait_recv()

        @pl.when(has_low)
        def _():
            arrived(0, k).wait_recv()

        @pl.when(has_high)
        def _():
            arrived(2, k).wait_recv()

        return 0

    def gather_sent(k, _):
        @pl.when(k > 0)
        def _():
            gather_copy(0, k).wait_send()

        @pl.when(has_low)
        def _():
            gather_copy(-1, k).wait_send()

        @pl.when(has_high)
        def _():
            gather_copy(1, k).wait_send()

        return 0

    lax.fori_loop(0, N, gather_start, 0)
    start(middle_v2)
    lax.fori_loop(0, N, gather_receive, 0)

    slab = pl.ds(8, cols)
    turned = [rolled(gvw[t, 0, slab, :], 64, 1) for t in (1, 2, 3)]
    for t in range(3):
        centre = gvw[t + 1, 0, slab, :]
        along_x = pair_x_sum(turned[max(t - 1, 0)], turned[t], turned[min(t + 1, 2)])
        along_y = gvw[t + 1, 0, pl.ds(7, cols), :] + gvw[t + 1, 0, pl.ds(9, cols), :]
        diagonal = gvw[t + 1, 1, slab, :]
        weight = jnp.where(diagonal > 0.0, OMEGA / diagonal, 0.0)
        t2[t, slab, :] = (1.0 + KEEP) * centre + weight * (along_x + along_y + z_sum(centre, 64))
    turned = [rolled(t2[t, slab, :], 64, 1) for t in range(3)]
    centre = t2[1, slab, :]
    gv2[2, slab, :] = centre
    diagonal = gvw[2, 1, slab, :]
    along_x = pair_x_sum(*turned)
    along_y = t2[1, pl.ds(7, cols), :] + t2[1, pl.ds(9, cols), :]
    rest = diagonal * (gvw[2, 0, slab, :] * (1.0 / OMEGA) - centre) + (along_x + along_y + z_sum(centre, 64))

    for load in loads[2:]:
        load.wait()
    along_z = dot(rest, common[pl.ds(0, 128), :])
    along_yz = dot(common[pl.ds(256, 4 * N), pl.ds(0, cols)], along_z)
    group = lanes_of(N) // 32
    mine = along_yz[0:N, :]
    for g in range(1, 4):
        mine = jnp.where(group == g, along_yz[g * N : (g + 1) * N, :], mine)
    modes[i, pl.ds(0, N), :] = mine
    modes[i, pl.ds(N, 1), :] = jnp.sum(diagonal - 6.0, axis=0, keepdims=True)

    def wide_copy(k):
        return pltpu.make_async_remote_copy(
            src_ref=modes.at[i], dst_ref=modes.at[i], send_sem=wide_send.at[k], recv_sem=wide_recv.at[i],
            device_id=(lax.rem(i + k, W), n), device_id_type=MESH,
        )

    def wide_start(k, _):
        wide_copy(k).start()
        return 0

    def wide_receive(k, _):
        other = lax.rem(i + k, W)
        pltpu.make_async_remote_copy(
            src_ref=modes.at[i], dst_ref=modes.at[other], send_sem=wide_send.at[0], recv_sem=wide_recv.at[other],
            device_id=(other, n), device_id_type=MESH,
        ).wait_recv()
        return 0

    def wide_sent(k, _):
        wide_copy(k).wait_send()
        return 0

    lax.fori_loop(1, W, wide_start, 0)
    start(coarse_far)
    receive(middle_v2)
    lax.fori_loop(1, W, wide_receive, 0)

    total = jnp.sum(modes[:, N, :], keepdims=True)
    mean = total * (1.0 / (2 * W * 8 * N * 64))
    shifted = common[pl.ds(256 + 4 * N, N), :] + mean
    sine_x, eigen_x = sine_table(W), sine_eigen(W)
    factor = (2.0 / (W + 1.0)) * (2.0 / (4 * N + 1.0)) * (2.0 / 33.0)
    half = W // 2
    even, odd = [], []
    for j in range(half):
        first, second = modes[j, pl.ds(0, N), :], modes[W - 1 - j, pl.ds(0, N), :]
        even.append(first + second)
        odd.append(first - second)
    found = [None] * 5
    for a in range(W):
        values = even if a % 2 == 0 else odd
        acc = None
        for j in range(half):
            term = values[j] * np.float32(sine_x[a, j])
            acc = term if acc is None else acc + term
        scaled = acc * np.float32(factor) / (shifted + np.float32(eigen_x[a]))
        for t in range(5):
            term = invx[t, pl.ds(a, 1), :] * scaled
            found[t] = term if found[t] is None else found[t] + term
    spread = dot(invy[:, pl.ds(0, N)], jnp.concatenate(found, axis=1))
    group = lanes_of(WINDOW) // 32
    parts = []
    for t in range(5):
        lanes = slice(128 * t, 128 * t + 128)
        part = spread[0:WINDOW, lanes]
        for g in range(1, 4):
            part = jnp.where(group == g, spread[g * WINDOW : (g + 1) * WINDOW, lanes], part)
        parts.append(part)
    correction = dot(jnp.concatenate(parts, axis=0), common[pl.ds(128, 128), :])

    receive(coarse_far)
    u = [gv2[t, window, :] + correction[WINDOW * t : WINDOW * (t + 1), :] for t in range(5)]

    def pair_sweep(u, slots):
        turned = {t: rolled(u[t], 64, 1) for t in u}
        swept = {}
        for t in slots:
            along_x = pair_x_sum(turned.get(t - 1, turned[t]), turned[t], turned.get(t + 1, turned[t]))
            along_y = rolled(u[t], 1, 0) + rolled(u[t], -1, 0)
            diagonal = gvw[t, 1, window, :]
            weight = jnp.where(diagonal > 0.0, OMEGA / diagonal, 0.0)
            summed = along_x + along_y + z_sum(u[t], 64)
            swept[t] = KEEP * u[t] + gvw[t, 0, window, :] + weight * summed
        return swept

    u = pair_sweep(dict(enumerate(u)), range(5))
    u = pair_sweep(u, range(1, 4))

    for t in (1, 2, 3):
        u2[t - 1, :, :] = u[t]
    for t in range(3):
        halves = spread_lanes(u2[t, pl.ds(4, 16), :])
        for h in range(2):
            for k in range(2):
                r = 4 * t + 2 * h + k
                ub1[r, pl.ds(0, 16, stride=2), :] = halves[h]
                ub1[r, pl.ds(1, 16, stride=2), :] = halves[h]
    for r in range(12):
        ub1[r, :, :] = ub1[r, :, :] + v2b[r, :, :]

    def middle_sweep(src, dst, r):
        centre, summed = middle_sum(src, r, 4, 24)
        part = (r, pl.ds(4, 24), slice(None))
        dst[part] = KEEP * centre + vb[part] + wb[part] * summed

    for r in range(1, 11):
        middle_sweep(ub1, ub2, r)
    for r in range(2, 10):
        middle_sweep(ub2, ub1, r)

    def fine_spread(q, _):
        halves = spread_lanes(ub1[q + 2, pl.ds(4, 24), :])
        for k in range(2):
            r = 2 * q + k
            for h in range(2):
                ua[r, h, pl.ds(0, 24, stride=2), :] = halves[h]
                ua[r, h, pl.ds(1, 24, stride=2), :] = halves[h]
        for k in range(2):
            r = 2 * q + k
            for h in range(2):
                ua[r, h, :, :] = ua[r, h, :, :] + v2a[r, h, :, :]
        return 0

    lax.fori_loop(0, 8, fine_spread, 0)

    def fine_sweep(src, dst, r, _):
        centre, summed = fine_sum(src, r, 4, 40)
        for h in range(2):
            part = (r, h, pl.ds(4, 40), slice(None))
            dst[part] = KEEP * centre[h] + va[part] + wa[part] * summed[h]
        return 0

    lax.fori_loop(2, 14, functools.partial(fine_sweep, ua, ub), 0)
    lax.fori_loop(3, 13, functools.partial(fine_sweep, ub, ua), 0)

    def fine_end(r, _):
        centre, summed = fine_sum(ua, r + 4, 8, 32)
        for h in range(2):
            lanes = pl.ds(128 * h, 128)
            out_v[r, :, lanes] = centre[h]
            res_v[r, :, lanes] = fine_residual(ua, r, h, centre[h], summed[h])
        return 0

    lax.fori_loop(0, 8, fine_end, 0)
    stores = [
        pltpu.make_async_copy(out_v, out_hbm, out_sem.at[0]),
        pltpu.make_async_copy(res_v, res_hbm, out_sem.at[1]),
    ]
    for store in stores:
        store.start()

    for pieces in (fine_near, fine_far, middle_w, middle_v, middle_v2, coarse_far):
        sent(pieces)
    lax.fori_loop(0, N, gather_sent, 0)
    lax.fori_loop(1, W, wide_sent, 0)
    for store in stores:
        store.wait()


def solution(mesh):
    W, N = mesh.shape["wide"], mesh.shape["narrow"]
    common, invx, invy = tables(W, N)
    cols = 8 * N
    vmem = pltpu.VMEM
    dma = pltpu.SemaphoreType.DMA
    fine, middle = (16, 2, 48, 128), (12, 32, 128)
    scratch = [
        vmem((8, 32, 256), F32), vmem((8, 32, 256), F32),
        vmem(common.shape, F32), vmem((5, W, 128), F32), vmem((4 * WINDOW, 128), F32),
        vmem((8, 32, 256), F32), vmem((8, 32, 256), F32),
        vmem(fine, F32), vmem(fine, F32), vmem(fine, F32), vmem(fine, F32), vmem(fine, F32),
        vmem((4, 2, 32, 128), F32),
        vmem(middle, F32), vmem(middle, F32), vmem(middle, F32), vmem(middle, F32),
        vmem(middle, F32), vmem(middle, F32),
        vmem((4, 16, 128), F32), vmem((4, 16, 128), F32), vmem((2, 16, 128), F32),
        vmem((5, 2, cols + 16, 128), F32), vmem((5, cols + 16, 128), F32),
        vmem((3, cols + 16, 128), F32), vmem((3, WINDOW, 128), F32),
        vmem((W, N + 1, 128), F32),
        dma((5,)), dma((2,)), dma((70,)), dma((70,)), dma((3, N)), dma((3, N)), dma((W,)), dma((W,)),
    ]

    def per_device(divergence, screening):
        block = jax.ShapeDtypeStruct((8, 32, 256), F32)
        anywhere = pl.BlockSpec(memory_space=pl.ANY)
        return pl.pallas_call(
            functools.partial(cycle_kernel, W, N),
            out_shape=(block, block),
            in_specs=[anywhere] * 5,
            out_specs=(anywhere, anywhere),
            scratch_shapes=scratch,
            compiler_params=pltpu.CompilerParams(
                collective_id=0, has_side_effects=True, vmem_limit_bytes=32 * 1024 * 1024
            ),
        )(divergence, screening, jnp.asarray(common), jnp.asarray(invx), jnp.asarray(invy))

    spec = P("wide", "narrow", None)
    return jax.shard_map(
        per_device, mesh=mesh, in_specs=(spec, spec), out_specs=(spec, spec), check_vma=False
    )
```

time: 604 us -> 54.5 us (0.09)
  the two profiles are of different devices: /device:TPU:160 before, /device:TPU:7 now
where the time goes in v1:
time: 54.5 us; the launch traced here: 54.2 us
  Pallas kernels  47.3 us (87%)
  local copies, waits for them, and re-layouts  6.27 us (12%)
  between operations  0.65 us (1%)
    pallas_call x1, Pallas kernels, per_device(): pl.pallas_call(functools.partial(cycle_kernel, W, N), out_shape=(block, b...  47.3 us
    unnamed x12, local copies, waits for them, and re-layouts  6.27 us

profile of v1, /device:TPU:7, one launch (start us, length us, event | category | flops | bytes accessed | tf_op | source)
XLA Modules:
  0.0 54.2 jit_solution(4064838049038968603)
XLA Ops:
  0.6 0.0 copy-start
  0.6 1.1 %copy-done = f32[36,32,128]{2,1,0:T(8,128)S(1)} copy-done((f32[36,32,128]{2,1,0:T(8,128)S(1)}, f32[36,32,128]{2,1,0:T(8,128)}, u32[]{:S(2)}) %copy-start) | copy-done | bytes 589848
  1.7 0.0 copy-start.1
  1.7 1.0 %copy-done.1 = f32[8,96,128]{2,1,0:T(8,128)S(1)} copy-done((f32[8,96,128]{2,1,0:T(8,128)S(1)}, f32[8,96,128]{2,1,0:T(8,128)}, u32[]{:S(2)}) %copy-start.1) | copy-done | bytes 393240
  2.7 0.0 copy-start.2
  2.7 0.9 %copy-done.2 = f32[8,32,256]{2,1,0:T(8,128)S(1)} copy-done((f32[8,32,256]{2,1,0:T(8,128)S(1)}, f32[8,32,256]{2,1,0:T(8,128)}, u32[]{:S(2)}) %copy-start.2) | copy-done | bytes 262168
  3.6 0.0 copy-start.3
  3.6 0.9 %copy-done.3 = f32[8,32,256]{2,1,0:T(8,128)S(1)} copy-done((f32[8,32,256]{2,1,0:T(8,128)S(1)}, f32[8,32,256]{2,1,0:T(8,128)}, u32[]{:S(2)}) %copy-start.3) | copy-done | bytes 262168
  4.6 0.0 copy-start.4
  4.6 0.9 %copy-done.4 = f32[296,128]{1,0:T(8,128)S(1)} copy-done((f32[296,128]{1,0:T(8,128)S(1)}, f32[296,128]{1,0:T(8,128)}, u32[]{:S(2)}) %copy-start.4) | copy-done | bytes 151576
  5.5 47.3 %shard_map.68 = (f32[8,32,256]{2,1,0:T(8,128)S(1)}, f32[8,32,256]{2,1,0:T(8,128)S(1)}) custom-call(f32[8,32,256]{2,1,0:T(8,128)S(1)} %copy-done.2, f32[8,32,256]{2,1,0:T(8,128)S(1)} %copy-done.3, f32[296,128]{1,0:T(8,128)S(1)} %copy-done.4, f32[36,32,128]{2,1,0:T(8,128)S(1)} %copy-done, f32[8,96,128]{2,1,0:T(8,128)S(1)} %copy-done.1), custom_call_target="tpu_custom_call" | custom-call | tf_op jit(solution)/shard_map/pallas_call | solution.py:680
  52.8 0.7 %copy.9 = f32[8,32,256]{2,1,0:T(8,128)} copy(f32[8,32,256]{2,1,0:T(8,128)S(1)} %get-tuple-element.4) | data formatting | bytes 524288
  53.5 0.7 %copy.10 = f32[8,32,256]{2,1,0:T(8,128)} copy(f32[8,32,256]{2,1,0:T(8,128)S(1)} %get-tuple-element.5) | data formatting | bytes 524288
Async XLA Ops:
  0.6 1.1 %copy-start = (f32[36,32,128]{2,1,0:T(8,128)S(1)}, f32[36,32,128]{2,1,0:T(8,128)}, u32[]{:S(2)}) copy-start(f32[36,32,128]{2,1,0:T(8,128)} %constant.7.clone.invx_hbm) | copy-start | bytes 1769476
  1.7 1.0 %copy-start.1 = (f32[8,96,128]{2,1,0:T(8,128)S(1)}, f32[8,96,128]{2,1,0:T(8,128)}, u32[]{:S(2)}) copy-start(f32[8,96,128]{2,1,0:T(8,128)} %constant.8.clone.invy_hbm) | copy-start | bytes 1179652
  2.7 0.9 %copy-start.2 = (f32[8,32,256]{2,1,0:T(8,128)S(1)}, f32[8,32,256]{2,1,0:T(8,128)}, u32[]{:S(2)}) copy-start(f32[8,32,256]{2,1,0:T(8,128)} %f_hbm.1) | copy-start | bytes 786436
  3.6 0.9 %copy-start.3 = (f32[8,32,256]{2,1,0:T(8,128)S(1)}, f32[8,32,256]{2,1,0:T(8,128)}, u32[]{:S(2)}) copy-start(f32[8,32,256]{2,1,0:T(8,128)} %s_hbm.1) | copy-start | bytes 786436
  4.6 0.9 %copy-start.4 = (f32[296,128]{1,0:T(8,128)S(1)}, f32[296,128]{1,0:T(8,128)}, u32[]{:S(2)}) copy-start(f32[296,128]{1,0:T(8,128)} %constant.6.clone.common_hbm) | copy-start | bytes 454660

commit v2 on v1

--- a/solution.py
+++ b/solution.py
@@ -138,117 +138,12 @@
             )
         )
     ]
-    for load in loads:
-        load.start()
-
     barrier = pltpu.get_barrier_semaphore()
 
     def greet(wide_id, narrow_id):
         pl.semaphore_signal(barrier, inc=1, device_id=(wide_id, narrow_id), device_id_type=MESH)
 
     has_low, has_high = i > 0, i < W - 1
-
-    def greet_narrow(k, _):
-        other = lax.rem(n + k, N)
-        greet(i, other)
-
-        @pl.when(has_low)
-        def _():
-            greet(i - 1, other)
-
-        @pl.when(has_high)
-        def _():
-            greet(i + 1, other)
-
-        return 0
-
-    lax.fori_loop(1, N, greet_narrow, 0)
-
-    def greet_wide(k, _):
-        greet(lax.rem(i + k, W), n)
-        return 0
-
-    lax.fori_loop(1, W, greet_wide, 0)
-
-    def zero(ref, *index):
-        shape = ref.at[index].shape if index else ref.shape
-        ref[index if index else ...] = jnp.zeros(shape, F32)
-
-    all_ = slice(None)
-
-    @pl.when(i == 0)
-    def _():
-        for ref in (va, wa):
-            zero(ref, pl.ds(0, 4))
-        for ref in (vb, wb, v2b):
-            zero(ref, pl.ds(0, 4))
-        zero(gvw, pl.ds(0, 2))
-        zero(gv2, pl.ds(0, 2))
-
-    @pl.when(i == W - 1)
-    def _():
-        for ref in (va, wa):
-            zero(ref, pl.ds(12, 4))
-        for ref in (vb, wb, v2b):
-            zero(ref, pl.ds(8, 4))
-        zero(gvw, pl.ds(3, 2))
-        zero(gv2, pl.ds(3, 2))
-
-    @pl.when(i == 1)
-    def _():
-        zero(gvw, 0)
-        zero(gv2, 0)
-
-    @pl.when(i == W - 2)
-    def _():
-        zero(gvw, 4)
-        zero(gv2, 4)
-
-    @pl.when(n == 0)
-    def _():
-        for ref in (va, wa):
-            zero(ref, all_, all_, pl.ds(0, 8))
-        for ref in (vb, wb, v2b):
-            zero(ref, all_, pl.ds(0, 8))
-
-    @pl.when(n == N - 1)
-    def _():
-        for ref in (va, wa):
-            zero(ref, all_, all_, pl.ds(40, 8))
-        for ref in (vb, wb, v2b):
-            zero(ref, all_, pl.ds(24, 8))
-
-    cols = 8 * N
-    zero(gvw, pl.ds(1, 3), all_, pl.ds(0, 8))
-    zero(gvw, pl.ds(1, 3), all_, pl.ds(8 + cols, 8))
-    zero(gv2, 2, pl.ds(0, 8))
-    zero(gv2, 2, pl.ds(8 + cols, 8))
-    zero(t2, all_, pl.ds(0, 8))
-    zero(t2, all_, pl.ds(8 + cols, 8))
-
-    loads[0].wait()
-    loads[1].wait()
-
-    def start_fine(r, _):
-        for h in range(2):
-            screen = s_in[r, :, pl.ds(128 * h, 128)]
-            weight = OMEGA / (6.0 + screen)
-            wa[r + 4, h, pl.ds(8, 32), :] = weight
-            va[r + 4, h, pl.ds(8, 32), :] = f_in[r, :, pl.ds(128 * h, 128)] * weight
-        return 0
-
-    lax.fori_loop(0, 8, start_fine, 0)
-
-    counter = [0]
-
-    def span(step, first, size, depths):
-        if step == 0:
-            return pl.ds(first, size), pl.ds(first, size)
-        low, high = depths
-        count = high - low + 1
-        if step > 0:
-            return pl.ds(first + size - high, count), pl.ds(first - high, count)
-        return pl.ds(first + low - 1, count), pl.ds(first + size + low - 1, count)
 
     def there(dx, dy):
         terms = []
@@ -262,6 +157,127 @@
             terms.append(n >= -dy)
         return functools.reduce(jnp.logical_and, terms)
 
+    sides = (-1, 1)
+    corners = [(dx, dy) for dx in sides for dy in sides]
+    for dx, dy in [(0, -1), (0, 1)] + corners + [(-1, 0), (1, 0)]:
+        pl.when(there(dx, dy))(functools.partial(greet, i + dx, n + dy))
+
+    for load in loads:
+        load.start()
+
+    def greet_narrow(k, _):
+        other = lax.rem(n + k, N)
+
+        @pl.when(jnp.logical_and(other != n - 1, other != n + 1))
+        def _():
+            greet_column(other)
+
+        return 0
+
+    def greet_column(other):
+        greet(i, other)
+
+        @pl.when(has_low)
+        def _():
+            greet(i - 1, other)
+
+        @pl.when(has_high)
+        def _():
+            greet(i + 1, other)
+
+    lax.fori_loop(1, N, greet_narrow, 0)
+
+    def greet_wide(k, _):
+        other = lax.rem(i + k, W)
+
+        @pl.when(jnp.logical_and(other != i - 1, other != i + 1))
+        def _():
+            greet(other, n)
+
+        return 0
+
+    lax.fori_loop(1, W, greet_wide, 0)
+
+    def zero(ref, *index):
+        shape = ref.at[index].shape if index else ref.shape
+        ref[index if index else ...] = jnp.zeros(shape, F32)
+
+    all_ = slice(None)
+
+    @pl.when(i == 0)
+    def _():
+        for ref in (va, wa):
+            zero(ref, pl.ds(0, 4))
+        for ref in (vb, wb, v2b):
+            zero(ref, pl.ds(0, 4))
+        zero(gvw, pl.ds(0, 2))
+        zero(gv2, pl.ds(0, 2))
+
+    @pl.when(i == W - 1)
+    def _():
+        for ref in (va, wa):
+            zero(ref, pl.ds(12, 4))
+        for ref in (vb, wb, v2b):
+            zero(ref, pl.ds(8, 4))
+        zero(gvw, pl.ds(3, 2))
+        zero(gv2, pl.ds(3, 2))
+
+    @pl.when(i == 1)
+    def _():
+        zero(gvw, 0)
+        zero(gv2, 0)
+
+    @pl.when(i == W - 2)
+    def _():
+        zero(gvw, 4)
+        zero(gv2, 4)
+
+    @pl.when(n == 0)
+    def _():
+        for ref in (va, wa):
+            zero(ref, all_, all_, pl.ds(0, 8))
+        for ref in (vb, wb, v2b):
+            zero(ref, all_, pl.ds(0, 8))
+
+    @pl.when(n == N - 1)
+    def _():
+        for ref in (va, wa):
+            zero(ref, all_, all_, pl.ds(40, 8))
+        for ref in (vb, wb, v2b):
+            zero(ref, all_, pl.ds(24, 8))
+
+    cols = 8 * N
+    zero(gvw, pl.ds(1, 3), all_, pl.ds(0, 8))
+    zero(gvw, pl.ds(1, 3), all_, pl.ds(8 + cols, 8))
+    zero(gv2, 2, pl.ds(0, 8))
+    zero(gv2, 2, pl.ds(8 + cols, 8))
+    zero(t2, all_, pl.ds(0, 8))
+    zero(t2, all_, pl.ds(8 + cols, 8))
+
+    loads[0].wait()
+    loads[1].wait()
+
+    def start_fine(r, _):
+        for h in range(2):
+            screen = s_in[r, :, pl.ds(128 * h, 128)]
+            weight = OMEGA / (6.0 + screen)
+            wa[r + 4, h, pl.ds(8, 32), :] = weight
+            va[r + 4, h, pl.ds(8, 32), :] = f_in[r, :, pl.ds(128 * h, 128)] * weight
+        return 0
+
+    lax.fori_loop(0, 8, start_fine, 0, unroll=True)
+
+    counter = [0]
+
+    def span(step, first, size, depths):
+        if step == 0:
+            return pl.ds(first, size), pl.ds(first, size)
+        low, high = depths
+        count = high - low + 1
+        if step > 0:
+            return pl.ds(first + size - high, count), pl.ds(first - high, count)
+        return pl.ds(first + low - 1, count), pl.ds(first + size + low - 1, count)
+
     def exchange(src, dst, dx, dy):
         k = counter[0]
         counter[0] += 1
@@ -280,9 +296,6 @@
         src_x, dst_x = span(dx, 4, 4, depth_x)
         src_y, dst_y = span(dy, 8, 16, depth_y)
         return exchange(ref.at[src_x, src_y, :], ref.at[dst_x, dst_y, :], dx, dy)
-
-    sides = (-1, 1)
-    corners = [(dx, dy) for dx in sides for dy in sides]
 
     def start(pieces):
         for copy, to, _ in pieces:
@@ -346,7 +359,7 @@
         wb[q + 4, pl.ds(8, 16), :] = OMEGA / diagonal
         return 0
 
-    lax.fori_loop(0, 4, screen_middle, 0)
+    lax.fori_loop(0, 4, screen_middle, 0, unroll=True)
     start(middle_w)
 
     for h in range(2):
@@ -356,6 +369,43 @@
     own_cols = pl.ds(pl.multiple_of(8 + 8 * n, 8), 8)
     gvw[2, 1, own_cols, :] = coarse_d
 
+    def gather_copy(what, dx, k):
+        other = lax.rem(n + k, N)
+        target = lax.rem(i + dx + W, W)
+        return pltpu.make_async_remote_copy(
+            src_ref=gvw.at[2, what, own_cols, :], dst_ref=gvw.at[2 - dx, what, own_cols, :],
+            send_sem=gather_send.at[what, dx + 1, k], recv_sem=gather_recv.at[what, 1 - dx, n],
+            device_id=(target, other), device_id_type=MESH,
+        )
+
+    def arrived(what, slot, k):
+        other = lax.rem(n + k, N)
+        cells = pl.ds(pl.multiple_of(8 + 8 * other, 8), 8)
+        return pltpu.make_async_remote_copy(
+            src_ref=gvw.at[2, what, own_cols, :], dst_ref=gvw.at[1 + slot, what, cells, :],
+            send_sem=gather_send.at[what, 0, 0], recv_sem=gather_recv.at[what, slot, other],
+            device_id=(lax.rem(i + 1, W), n), device_id_type=MESH,
+        )
+
+    def for_each(k, call):
+        pl.when(k > 0)(functools.partial(call, 0))
+        pl.when(has_low)(functools.partial(call, -1))
+        pl.when(has_high)(functools.partial(call, 1))
+
+    def gather_start(what, k, _):
+        for_each(k, lambda dx: gather_copy(what, dx, k).start())
+        return 0
+
+    def gather_receive(what, k, _):
+        for_each(k, lambda dx: arrived(what, 1 + dx, k).wait_recv())
+        return 0
+
+    def gather_sent(what, k, _):
+        for_each(k, lambda dx: gather_copy(what, dx, k).wait_send())
+        return 0
+
+    lax.fori_loop(0, N, functools.partial(gather_start, 1), 0)
+
     def fine_v2(a, count, r, _):
         centre, summed = fine_sum(va, r, a, count)
         for h in range(2):
@@ -364,7 +414,7 @@
 
     receive(fine_near)
     fine_v2(8, 32, 3, 0)
-    lax.fori_loop(4, 12, functools.partial(fine_v2, 7, 34), 0)
+    lax.fori_loop(4, 12, functools.partial(fine_v2, 7, 34), 0, unroll=True)
     fine_v2(8, 32, 12, 0)
 
     def fine_residual(ref, r, h, centre, summed):
@@ -386,11 +436,11 @@
         vb[q + 4, pl.ds(8, 16), :] = source * wb[q + 4, pl.ds(8, 16), :]
         return 0
 
-    lax.fori_loop(0, 4, fine_down, 0)
+    lax.fori_loop(0, 4, fine_down, 0, unroll=True)
     start(middle_v)
 
     receive(fine_far)
-    lax.fori_loop(1, 15, functools.partial(fine_v2, 4, 40), 0)
+    lax.fori_loop(1, 15, functools.partial(fine_v2, 4, 40), 0, unroll=True)
 
     receive(middle_w)
     receive(middle_v)
@@ -408,72 +458,10 @@
     low, high = (foldb[h, pl.ds(0, 8, stride=2), :] + foldb[h, pl.ds(1, 8, stride=2), :] for h in range(2))
     gvw[2, 0, own_cols, :] = 0.5 * fold_lanes(low, high) * (OMEGA / coarse_d)
 
-    def gather_copy(dx, k):
-        other = lax.rem(n + k, N)
-        target = lax.rem(i + dx + W, W)
-        return pltpu.make_async_remote_copy(
-            src_ref=gvw.at[2, :, own_cols, :], dst_ref=gvw.at[2 - dx, :, own_cols, :],
-            send_sem=gather_send.at[dx + 1, k], recv_sem=gather_recv.at[1 - dx, n],
-            device_id=(target, other), device_id_type=MESH,
-        )
-
-    def arrived(slot, k):
-        other = lax.rem(n + k, N)
-        cells = pl.ds(pl.multiple_of(8 + 8 * other, 8), 8)
-        return pltpu.make_async_remote_copy(
-            src_ref=gvw.at[2, :, own_cols, :], dst_ref=gvw.at[1 + slot, :, cells, :],
-            send_sem=gather_send.at[0, 0], recv_sem=gather_recv.at[slot, other],
-            device_id=(lax.rem(i + 1, W), n), device_id_type=MESH,
-        )
-
-    def gather_start(k, _):
-        @pl.when(k > 0)
-        def _():
-            gather_copy(0, k).start()
-
-        @pl.when(has_low)
-        def _():
-            gather_copy(-1, k).start()
-
-        @pl.when(has_high)
-        def _():
-            gather_copy(1, k).start()
-
-        return 0
-
-    def gather_receive(k, _):
-        @pl.when(k > 0)
-        def _():
-            arrived(1, k).wait_recv()
-
-        @pl.when(has_low)
-        def _():
-            arrived(0, k).wait_recv()
-
-        @pl.when(has_high)
-        def _():
-            arrived(2, k).wait_recv()
-
-        return 0
-
-    def gather_sent(k, _):
-        @pl.when(k > 0)
-        def _():
-            gather_copy(0, k).wait_send()
-
-        @pl.when(has_low)
-        def _():
-            gather_copy(-1, k).wait_send()
-
-        @pl.when(has_high)
-        def _():
-            gather_copy(1, k).wait_send()
-
-        return 0
-
-    lax.fori_loop(0, N, gather_start, 0)
+    lax.fori_loop(0, N, functools.partial(gather_start, 0), 0)
     start(middle_v2)
-    lax.fori_loop(0, N, gather_receive, 0)
+    lax.fori_loop(0, N, functools.partial(gather_receive, 1), 0)
+    lax.fori_loop(0, N, functools.partial(gather_receive, 0), 0)
 
     slab = pl.ds(8, cols)
     turned = [rolled(gvw[t, 0, slab, :], 64, 1) for t in (1, 2, 3)]
@@ -527,6 +515,10 @@
 
     lax.fori_loop(1, W, wide_start, 0)
     start(coarse_far)
+    for pieces in (fine_near, fine_far, middle_w, middle_v, middle_v2):
+        sent(pieces)
+    for what in range(2):
+        lax.fori_loop(0, N, functools.partial(gather_sent, what), 0)
     receive(middle_v2)
     lax.fori_loop(1, W, wide_receive, 0)
 
@@ -616,7 +608,7 @@
                 ua[r, h, :, :] = ua[r, h, :, :] + v2a[r, h, :, :]
         return 0
 
-    lax.fori_loop(0, 8, fine_spread, 0)
+    lax.fori_loop(0, 8, fine_spread, 0, unroll=True)
 
     def fine_sweep(src, dst, r, _):
         centre, summed = fine_sum(src, r, 4, 40)
@@ -625,8 +617,8 @@
             dst[part] = KEEP * centre[h] + va[part] + wa[part] * summed[h]
         return 0
 
-    lax.fori_loop(2, 14, functools.partial(fine_sweep, ua, ub), 0)
-    lax.fori_loop(3, 13, functools.partial(fine_sweep, ub, ua), 0)
+    lax.fori_loop(2, 14, functools.partial(fine_sweep, ua, ub), 0, unroll=True)
+    lax.fori_loop(3, 13, functools.partial(fine_sweep, ub, ua), 0, unroll=True)
 
     def fine_end(r, _):
         centre, summed = fine_sum(ua, r + 4, 8, 32)
@@ -636,7 +628,7 @@
             res_v[r, :, lanes] = fine_residual(ua, r, h, centre[h], summed[h])
         return 0
 
-    lax.fori_loop(0, 8, fine_end, 0)
+    lax.fori_loop(0, 8, fine_end, 0, unroll=True)
     stores = [
         pltpu.make_async_copy(out_v, out_hbm, out_sem.at[0]),
         pltpu.make_async_copy(res_v, res_hbm, out_sem.at[1]),
@@ -644,9 +636,7 @@
     for store in stores:
         store.start()
 
-    for pieces in (fine_near, fine_far, middle_w, middle_v, middle_v2, coarse_far):
-        sent(pieces)
-    lax.fori_loop(0, N, gather_sent, 0)
+    sent(coarse_far)
     lax.fori_loop(1, W, wide_sent, 0)
     for store in stores:
         store.wait()
@@ -671,7 +661,7 @@
         vmem((5, 2, cols + 16, 128), F32), vmem((5, cols + 16, 128), F32),
         vmem((3, cols + 16, 128), F32), vmem((3, WINDOW, 128), F32),
         vmem((W, N + 1, 128), F32),
-        dma((5,)), dma((2,)), dma((70,)), dma((70,)), dma((3, N)), dma((3, N)), dma((W,)), dma((W,)),
+        dma((5,)), dma((2,)), dma((70,)), dma((70,)), dma((2, 3, N)), dma((2, 3, N)), dma((W,)), dma((W,)),
     ]
 
     def per_device(divergence, screening):
@@ -680,7 +670,7 @@
         return pl.pallas_call(
             functools.partial(cycle_kernel, W, N),
             out_shape=(block, block),
-            in_specs=[anywhere] * 5,
+            in_specs=[pl.BlockSpec(memory_space=pltpu.HBM)] * 5,
             out_specs=(anywhere, anywhere),
             scratch_shapes=scratch,
             compiler_params=pltpu.CompilerParams(

time: 54.5 us -> 49.2 us (0.903)
  Pallas kernels: 47.3 us -> 41.9 us
    pallas_call x1, Pallas kernels: 47.3 us -> 41.9 us  [per_device(): pl.pallas_call(functools.partial(cycle_kernel, W, N), out_shape=(block, b...]
where the time goes in v2:
time: 49.2 us; the launch traced here: 48.8 us
  Pallas kernels  41.9 us (85%)
  local copies, waits for them, and re-layouts  6.27 us (13%)
  between operations  0.65 us (1%)
    pallas_call x1, Pallas kernels, per_device(): pl.pallas_call(functools.partial(cycle_kernel, W, N), out_shape=(block, b...  41.9 us
    unnamed x12, local copies, waits for them, and re-layouts  6.27 us

profile of v2, /device:TPU:7, one launch (start us, length us, event | category | flops | bytes accessed | tf_op | source)
XLA Modules:
  0.0 48.8 jit_solution(9081902938162561307)
XLA Ops:
  0.6 0.0 copy-start
  0.6 1.1 %copy-done = f32[36,32,128]{2,1,0:T(8,128)S(1)} copy-done((f32[36,32,128]{2,1,0:T(8,128)S(1)}, f32[36,32,128]{2,1,0:T(8,128)}, u32[]{:S(2)}) %copy-start) | copy-done | bytes 589848
  1.7 0.0 copy-start.1
  1.7 1.0 %copy-done.1 = f32[8,96,128]{2,1,0:T(8,128)S(1)} copy-done((f32[8,96,128]{2,1,0:T(8,128)S(1)}, f32[8,96,128]{2,1,0:T(8,128)}, u32[]{:S(2)}) %copy-start.1) | copy-done | bytes 393240
  2.7 0.0 copy-start.2
  2.7 0.9 %copy-done.2 = f32[8,32,256]{2,1,0:T(8,128)S(1)} copy-done((f32[8,32,256]{2,1,0:T(8,128)S(1)}, f32[8,32,256]{2,1,0:T(8,128)}, u32[]{:S(2)}) %copy-start.2) | copy-done | bytes 262168
  3.6 0.0 copy-start.3
  3.6 0.9 %copy-done.3 = f32[8,32,256]{2,1,0:T(8,128)S(1)} copy-done((f32[8,32,256]{2,1,0:T(8,128)S(1)}, f32[8,32,256]{2,1,0:T(8,128)}, u32[]{:S(2)}) %copy-start.3) | copy-done | bytes 262168
  4.6 0.0 copy-start.4
  4.6 0.9 %copy-done.4 = f32[296,128]{1,0:T(8,128)S(1)} copy-done((f32[296,128]{1,0:T(8,128)S(1)}, f32[296,128]{1,0:T(8,128)}, u32[]{:S(2)}) %copy-start.4) | copy-done | bytes 151576
  5.5 41.9 %shard_map.68 = (f32[8,32,256]{2,1,0:T(8,128)S(1)}, f32[8,32,256]{2,1,0:T(8,128)S(1)}) custom-call(f32[8,32,256]{2,1,0:T(8,128)S(1)} %copy-done.2, f32[8,32,256]{2,1,0:T(8,128)S(1)} %copy-done.3, f32[296,128]{1,0:T(8,128)S(1)} %copy-done.4, f32[36,32,128]{2,1,0:T(8,128)S(1)} %copy-done, f32[8,96,128]{2,1,0:T(8,128)S(1)} %copy-done.1), custom_call_target="tpu_custom_call" | custom-call | tf_op jit(solution)/shard_map/pallas_call | solution.py:670
  47.4 0.7 %copy.9 = f32[8,32,256]{2,1,0:T(8,128)} copy(f32[8,32,256]{2,1,0:T(8,128)S(1)} %get-tuple-element.4) | data formatting | bytes 524288
  48.1 0.7 %copy.10 = f32[8,32,256]{2,1,0:T(8,128)} copy(f32[8,32,256]{2,1,0:T(8,128)S(1)} %get-tuple-element.5) | data formatting | bytes 524288
Async XLA Ops:
  0.6 1.1 %copy-start = (f32[36,32,128]{2,1,0:T(8,128)S(1)}, f32[36,32,128]{2,1,0:T(8,128)}, u32[]{:S(2)}) copy-start(f32[36,32,128]{2,1,0:T(8,128)} %constant.7.clone.invx_hbm) | copy-start | bytes 1769476
  1.7 1.0 %copy-start.1 = (f32[8,96,128]{2,1,0:T(8,128)S(1)}, f32[8,96,128]{2,1,0:T(8,128)}, u32[]{:S(2)}) copy-start(f32[8,96,128]{2,1,0:T(8,128)} %constant.8.clone.invy_hbm) | copy-start | bytes 1179652
  2.7 0.9 %copy-start.2 = (f32[8,32,256]{2,1,0:T(8,128)S(1)}, f32[8,32,256]{2,1,0:T(8,128)}, u32[]{:S(2)}) copy-start(f32[8,32,256]{2,1,0:T(8,128)} %f_hbm.1) | copy-start | bytes 786436
  3.6 0.9 %copy-start.3 = (f32[8,32,256]{2,1,0:T(8,128)S(1)}, f32[8,32,256]{2,1,0:T(8,128)}, u32[]{:S(2)}) copy-start(f32[8,32,256]{2,1,0:T(8,128)} %s_hbm.1) | copy-start | bytes 786436
  4.6 0.9 %copy-start.4 = (f32[296,128]{1,0:T(8,128)S(1)}, f32[296,128]{1,0:T(8,128)}, u32[]{:S(2)}) copy-start(f32[296,128]{1,0:T(8,128)} %constant.6.clone.common_hbm) | copy-start | bytes 454660

commit v3 on v2

--- a/solution.py
+++ b/solution.py
@@ -115,13 +115,13 @@
 def cycle_kernel(
     W, N,
     f_hbm, s_hbm, common_hbm, invx_hbm, invy_hbm,
-    out_hbm, res_hbm,
-    f_in, s_in, common, invx, invy, out_v, res_v,
+    out_v, res_v,
+    f_in, s_in, common, invx, invy,
     va, wa, v2a, ua, ub, fold,
     vb, wb, v2b, tb, ub1, ub2, fb, db, foldb,
     gvw, gv2, t2, u2,
     modes,
-    in_sem, out_sem, send_sem, recv_sem, gather_send, gather_recv, wide_send, wide_recv,
+    in_sem, send_sem, recv_sem, gather_send, gather_recv, wide_send, wide_recv,
 ):
     i = lax.axis_index("wide")
     n = lax.axis_index("narrow")
@@ -629,17 +629,8 @@
         return 0
 
     lax.fori_loop(0, 8, fine_end, 0, unroll=True)
-    stores = [
-        pltpu.make_async_copy(out_v, out_hbm, out_sem.at[0]),
-        pltpu.make_async_copy(res_v, res_hbm, out_sem.at[1]),
-    ]
-    for store in stores:
-        store.start()
-
     sent(coarse_far)
     lax.fori_loop(1, W, wide_sent, 0)
-    for store in stores:
-        store.wait()
 
 
 def solution(mesh):
@@ -652,7 +643,6 @@
     scratch = [
         vmem((8, 32, 256), F32), vmem((8, 32, 256), F32),
         vmem(common.shape, F32), vmem((5, W, 128), F32), vmem((4 * WINDOW, 128), F32),
-        vmem((8, 32, 256), F32), vmem((8, 32, 256), F32),
         vmem(fine, F32), vmem(fine, F32), vmem(fine, F32), vmem(fine, F32), vmem(fine, F32),
         vmem((4, 2, 32, 128), F32),
         vmem(middle, F32), vmem(middle, F32), vmem(middle, F32), vmem(middle, F32),
@@ -661,20 +651,19 @@
         vmem((5, 2, cols + 16, 128), F32), vmem((5, cols + 16, 128), F32),
         vmem((3, cols + 16, 128), F32), vmem((3, WINDOW, 128), F32),
         vmem((W, N + 1, 128), F32),
-        dma((5,)), dma((2,)), dma((70,)), dma((70,)), dma((2, 3, N)), dma((2, 3, N)), dma((W,)), dma((W,)),
+        dma((5,)), dma((70,)), dma((70,)), dma((2, 3, N)), dma((2, 3, N)), dma((W,)), dma((W,)),
     ]
 
     def per_device(divergence, screening):
-        block = jax.ShapeDtypeStruct((8, 32, 256), F32)
-        anywhere = pl.BlockSpec(memory_space=pl.ANY)
+        block = pltpu.VMEM((8, 32, 256), F32)
         return pl.pallas_call(
             functools.partial(cycle_kernel, W, N),
             out_shape=(block, block),
             in_specs=[pl.BlockSpec(memory_space=pltpu.HBM)] * 5,
-            out_specs=(anywhere, anywhere),
+            out_specs=(pl.BlockSpec(memory_space=pltpu.VMEM),) * 2,
             scratch_shapes=scratch,
             compiler_params=pltpu.CompilerParams(
-                collective_id=0, has_side_effects=True, vmem_limit_bytes=32 * 1024 * 1024
+                collective_id=0, has_side_effects=True, vmem_limit_bytes=56 * 1024 * 1024
             ),
         )(divergence, screening, jnp.asarray(common), jnp.asarray(invx), jnp.asarray(invy))
 

time: 49.2 us -> 44 us (0.89)
  local copies, waits for them, and re-layouts: 6.27 us -> 1.41 us
    unnamed x12 -> x2, local copies, waits for them, and re-layouts: 6.27 us -> 1.41 us
where the time goes in v3:
time: 44 us; the launch traced here: 43.7 us
  Pallas kernels  41.7 us (95%)
  local copies, waits for them, and re-layouts  1.41 us (3%)
  between operations  0.64 us (1%)
    pallas_call x1, Pallas kernels, per_device(): pl.pallas_call(functools.partial(cycle_kernel, W, N), out_shape=(block, b...  41.7 us
    unnamed x2, local copies, waits for them, and re-layouts  1.41 us

profile of v3, /device:TPU:7, one launch (start us, length us, event | category | flops | bytes accessed | tf_op | source)
XLA Modules:
  0.0 43.7 jit_solution(17111882238580684440)
XLA Ops:
  0.6 41.7 %shard_map.68 = (f32[8,32,256]{2,1,0:T(8,128)S(1)}, f32[8,32,256]{2,1,0:T(8,128)S(1)}) custom-call(f32[8,32,256]{2,1,0:T(8,128)} %f_hbm.1, f32[8,32,256]{2,1,0:T(8,128)} %s_hbm.1, f32[296,128]{1,0:T(8,128)} %constant.6.clone.common_hbm, f32[36,32,128]{2,1,0:T(8,128)} %constant.7.clone.invx_hbm, f32[8,96,128]{2,1,0:T(8,128)} %constant.8.clone.invy_hbm), custom_call_target="tpu_custom_call" | custom-call | tf_op jit(solution)/shard_map/pallas_call | solution.py:659
  42.3 0.7 %copy.9 = f32[8,32,256]{2,1,0:T(8,128)} copy(f32[8,32,256]{2,1,0:T(8,128)S(1)} %get-tuple-element.2) | data formatting | bytes 524288
  43.0 0.7 %copy.10 = f32[8,32,256]{2,1,0:T(8,128)} copy(f32[8,32,256]{2,1,0:T(8,128)S(1)} %get-tuple-element.3) | data formatting | bytes 524288

commit v4 on v3

--- a/solution.py
+++ b/solution.py
@@ -120,14 +120,14 @@
     va, wa, v2a, ua, ub, fold,
     vb, wb, v2b, tb, ub1, ub2, fb, db, foldb,
     gvw, gv2, t2, u2,
-    modes,
-    in_sem, send_sem, recv_sem, gather_send, gather_recv, wide_send, wide_recv,
+    modes, tally,
+    in_sem, send_sem, recv_sem, far_send, far_recv, gather_send, gather_recv, wide_send, wide_recv,
 ):
     i = lax.axis_index("wide")
     n = lax.axis_index("narrow")
 
     loads = [
-        pltpu.make_async_copy(src, dst, in_sem.at[k])
+        pltpu.make_async_copy(src, dst, in_sem.at[min(k, 2)])
         for k, (src, dst) in enumerate(
             (
                 (s_hbm, s_in),
@@ -267,7 +267,17 @@
 
     lax.fori_loop(0, 8, start_fine, 0, unroll=True)
 
-    counter = [0]
+    directions = [(0, -1), (0, 1)] + corners + [(-1, 0), (1, 0)]
+    rows_of = {}
+
+    def waiter(rows, send, recv, to):
+        part = tally.at[pl.ds(0, rows), :]
+        return pltpu.make_async_remote_copy(
+            src_ref=part, dst_ref=part, send_sem=send, recv_sem=recv, device_id=to, device_id_type=MESH
+        )
+
+    def beside(dx, dy):
+        return lax.rem(i + dx + W, W), lax.rem(n + dy + N, N)
 
     def span(step, first, size, depths):
         if step == 0:
@@ -278,68 +288,92 @@
             return pl.ds(first + size - high, count), pl.ds(first - high, count)
         return pl.ds(first + low - 1, count), pl.ds(first + size + low - 1, count)
 
-    def exchange(src, dst, dx, dy):
-        k = counter[0]
-        counter[0] += 1
+    def exchange(family, src, dst, dx, dy):
+        d = directions.index((dx, dy))
+        rows_of[family, d] = rows_of.get((family, d), 0) + int(np.prod(src.shape)) // 128
         copy = pltpu.make_async_remote_copy(
-            src_ref=src, dst_ref=dst, send_sem=send_sem.at[k], recv_sem=recv_sem.at[k],
-            device_id=(lax.rem(i + dx + W, W), lax.rem(n + dy + N, N)), device_id_type=MESH,
-        )
-        return copy, there(dx, dy), there(-dx, -dy)
-
-    def fine_piece(ref, dx, dy, depth_x=None, depth_y=None):
+            src_ref=src, dst_ref=dst, send_sem=send_sem.at[d], recv_sem=recv_sem.at[family, d],
+            device_id=beside(dx, dy), device_id_type=MESH,
+        )
+        return copy, there(dx, dy)
+
+    def fine_piece(family, ref, dx, dy, depth_x=None, depth_y=None):
         src_x, dst_x = span(dx, 4, 8, depth_x)
         src_y, dst_y = span(dy, 8, 32, depth_y)
-        return exchange(ref.at[src_x, :, src_y, :], ref.at[dst_x, :, dst_y, :], dx, dy)
-
-    def middle_piece(ref, dx, dy, depth_x=None, depth_y=None):
+        return exchange(family, ref.at[src_x, :, src_y, :], ref.at[dst_x, :, dst_y, :], dx, dy)
+
+    def middle_piece(family, ref, dx, dy, depth_x=None, depth_y=None):
         src_x, dst_x = span(dx, 4, 4, depth_x)
         src_y, dst_y = span(dy, 8, 16, depth_y)
-        return exchange(ref.at[src_x, src_y, :], ref.at[dst_x, dst_y, :], dx, dy)
+        return exchange(family, ref.at[src_x, src_y, :], ref.at[dst_x, dst_y, :], dx, dy)
 
     def start(pieces):
-        for copy, to, _ in pieces:
+        for copy, to in pieces:
             pl.when(to)(copy.start)
 
-    def receive(pieces):
-        for copy, _, come in pieces:
-            pl.when(come)(copy.wait_recv)
-
-    def sent(pieces):
-        for copy, to, _ in pieces:
-            pl.when(to)(copy.wait_send)
+    def receive(family):
+        for d, (dx, dy) in enumerate(directions):
+            arrival = waiter(rows_of[family, d], send_sem.at[d], recv_sem.at[family, d], beside(dx, dy))
+            pl.when(there(-dx, -dy))(arrival.wait_recv)
+
+    def halo_sent():
+        for d, (dx, dy) in enumerate(directions):
+            rows = sum(rows_of[family, d] for family in range(4))
+            pl.when(there(dx, dy))(waiter(rows, send_sem.at[d], recv_sem.at[0, d], beside(dx, dy)).wait_send)
 
     fine_near = (
-        [fine_piece(va, 0, d, None, (1, 2)) for d in sides]
-        + [fine_piece(wa, 0, d, None, (1, 1)) for d in sides]
-        + [fine_piece(va, dx, dy, (1, 1), (1, 1)) for dx, dy in corners]
-        + [fine_piece(va, d, 0, (1, 2)) for d in sides]
-        + [fine_piece(wa, d, 0, (1, 1)) for d in sides]
+        [fine_piece(0, va, 0, d, None, (1, 2)) for d in sides]
+        + [fine_piece(0, wa, 0, d, None, (1, 1)) for d in sides]
+        + [fine_piece(0, va, dx, dy, (1, 1), (1, 1)) for dx, dy in corners]
+        + [fine_piece(0, va, d, 0, (1, 2)) for d in sides]
+        + [fine_piece(0, wa, d, 0, (1, 1)) for d in sides]
     )
     fine_far = (
-        [fine_piece(va, 0, d, None, (3, 4)) for d in sides]
-        + [fine_piece(wa, 0, d, None, (2, 3)) for d in sides]
-        + [fine_piece(va, dx, dy, (1, 1), (2, 3)) for dx, dy in corners]
-        + [fine_piece(va, dx, dy, (2, 3), (1, 2)) for dx, dy in corners]
-        + [fine_piece(wa, dx, dy, (1, 2), (1, 2)) for dx, dy in corners]
-        + [fine_piece(va, d, 0, (3, 4)) for d in sides]
-        + [fine_piece(wa, d, 0, (2, 3)) for d in sides]
+        [fine_piece(1, va, 0, d, None, (3, 4)) for d in sides]
+        + [fine_piece(1, wa, 0, d, None, (2, 3)) for d in sides]
+        + [fine_piece(1, va, dx, dy, (1, 1), (2, 3)) for dx, dy in corners]
+        + [fine_piece(1, va, dx, dy, (2, 3), (1, 2)) for dx, dy in corners]
+        + [fine_piece(1, wa, dx, dy, (1, 2), (1, 2)) for dx, dy in corners]
+        + [fine_piece(1, va, d, 0, (3, 4)) for d in sides]
+        + [fine_piece(1, wa, d, 0, (2, 3)) for d in sides]
     )
 
-    def middle_pieces(ref, depth, corner):
+    def middle_pieces(family, ref, depth, corner):
         return (
-            [middle_piece(ref, 0, d, None, (1, depth)) for d in sides]
-            + [middle_piece(ref, dx, dy, (1, corner), (1, corner)) for dx, dy in corners]
-            + [middle_piece(ref, d, 0, (1, depth)) for d in sides]
-        )
-
-    middle_w = middle_pieces(wb, 3, 2)
-    middle_v = middle_pieces(vb, 3, 2)
-    middle_v2 = middle_pieces(v2b, 4, 3)
+            [middle_piece(family, ref, 0, d, None, (1, depth)) for d in sides]
+            + [middle_piece(family, ref, dx, dy, (1, corner), (1, corner)) for dx, dy in corners]
+            + [middle_piece(family, ref, d, 0, (1, depth)) for d in sides]
+        )
+
+    middle_w = middle_pieces(2, wb, 3, 2)
+    middle_v = middle_pieces(2, vb, 3, 2)
+    middle_v2 = middle_pieces(3, v2b, 4, 3)
 
     window = pl.ds(pl.multiple_of(8 * n, 8), WINDOW)
-    coarse_far = [exchange(gv2.at[2, window, :], gv2.at[2 - d, window, :], d, 0) for d in (-1, 1, -2, 2)]
-    coarse_far += [exchange(gvw.at[2, :, window, :], gvw.at[2 - d, :, window, :], d, 0) for d in (-2, 2)]
+    reach = (-2, -1, 1, 2)
+
+    def coarse_far(d):
+        k = reach.index(d)
+        args = dict(
+            send_sem=far_send.at[k], recv_sem=far_recv.at[k], device_id=beside(d, 0), device_id_type=MESH
+        )
+        copies = [pltpu.make_async_remote_copy(src_ref=gv2.at[2, window, :], dst_ref=gv2.at[2 - d, window, :], **args)]
+        if abs(d) == 2:
+            copies.append(
+                pltpu.make_async_remote_copy(
+                    src_ref=gvw.at[2, :, window, :], dst_ref=gvw.at[2 - d, :, window, :], **args
+                )
+            )
+        return copies
+
+    def coarse_far_start():
+        for d in reach:
+            for copy in coarse_far(d):
+                pl.when(there(d, 0))(copy.start)
+
+    def coarse_far_waiter(d):
+        k = reach.index(d)
+        return waiter((3 if abs(d) == 2 else 1) * WINDOW, far_send.at[k], far_recv.at[k], beside(d, 0))
 
     greeted = (W - 1) + (N - 1) * (1 + has_low.astype(jnp.int32) + has_high.astype(jnp.int32))
     pl.semaphore_wait(barrier, greeted)
@@ -374,18 +408,14 @@
         target = lax.rem(i + dx + W, W)
         return pltpu.make_async_remote_copy(
             src_ref=gvw.at[2, what, own_cols, :], dst_ref=gvw.at[2 - dx, what, own_cols, :],
-            send_sem=gather_send.at[what, dx + 1, k], recv_sem=gather_recv.at[what, 1 - dx, n],
+            send_sem=gather_send.at[what, dx + 1], recv_sem=gather_recv.at[what, 1 - dx],
             device_id=(target, other), device_id_type=MESH,
         )
 
-    def arrived(what, slot, k):
-        other = lax.rem(n + k, N)
-        cells = pl.ds(pl.multiple_of(8 + 8 * other, 8), 8)
-        return pltpu.make_async_remote_copy(
-            src_ref=gvw.at[2, what, own_cols, :], dst_ref=gvw.at[1 + slot, what, cells, :],
-            send_sem=gather_send.at[what, 0, 0], recv_sem=gather_recv.at[what, slot, other],
-            device_id=(lax.rem(i + 1, W), n), device_id_type=MESH,
-        )
+    def gather_waiter(what, dx):
+        rows = 8 * (N if dx else N - 1)
+        target = (lax.rem(i + 1, W), n)
+        return waiter(rows, gather_send.at[what, dx + 1], gather_recv.at[what, dx + 1], target)
 
     def for_each(k, call):
         pl.when(k > 0)(functools.partial(call, 0))
@@ -396,13 +426,11 @@
         for_each(k, lambda dx: gather_copy(what, dx, k).start())
         return 0
 
-    def gather_receive(what, k, _):
-        for_each(k, lambda dx: arrived(what, 1 + dx, k).wait_recv())
-        return 0
-
-    def gather_sent(what, k, _):
-        for_each(k, lambda dx: gather_copy(what, dx, k).wait_send())
-        return 0
+    def gather_receive(what):
+        for_each(1, lambda dx: gather_waiter(what, dx).wait_recv())
+
+    def gather_sent(what):
+        for_each(1, lambda dx: gather_waiter(what, dx).wait_send())
 
     lax.fori_loop(0, N, functools.partial(gather_start, 1), 0)
 
@@ -412,7 +440,7 @@
             v2a[r, h, pl.ds(a, count), :] = (1.0 + KEEP) * centre[h] + wa[r, h, pl.ds(a, count), :] * summed[h]
         return 0
 
-    receive(fine_near)
+    receive(0)
     fine_v2(8, 32, 3, 0)
     lax.fori_loop(4, 12, functools.partial(fine_v2, 7, 34), 0, unroll=True)
     fine_v2(8, 32, 12, 0)
@@ -439,11 +467,10 @@
     lax.fori_loop(0, 4, fine_down, 0, unroll=True)
     start(middle_v)
 
-    receive(fine_far)
+    receive(1)
     lax.fori_loop(1, 15, functools.partial(fine_v2, 4, 40), 0, unroll=True)
 
-    receive(middle_w)
-    receive(middle_v)
+    receive(2)
     for r in range(3, 9):
         centre, summed = middle_sum(vb, r, 4, 24)
         tb[r, pl.ds(4, 24), :] = (1.0 + KEEP) * centre + wb[r, pl.ds(4, 24), :] * summed
@@ -460,8 +487,8 @@
 
     lax.fori_loop(0, N, functools.partial(gather_start, 0), 0)
     start(middle_v2)
-    lax.fori_loop(0, N, functools.partial(gather_receive, 1), 0)
-    lax.fori_loop(0, N, functools.partial(gather_receive, 0), 0)
+    gather_receive(1)
+    gather_receive(0)
 
     slab = pl.ds(8, cols)
     turned = [rolled(gvw[t, 0, slab, :], 64, 1) for t in (1, 2, 3)]
@@ -480,8 +507,9 @@
     along_y = t2[1, pl.ds(7, cols), :] + t2[1, pl.ds(9, cols), :]
     rest = diagonal * (gvw[2, 0, slab, :] * (1.0 / OMEGA) - centre) + (along_x + along_y + z_sum(centre, 64))
 
-    for load in loads[2:]:
-        load.wait()
+    sizes = (common, invx, invy)
+    part = tally.at[pl.ds(0, sum(int(np.prod(ref.shape)) // 128 for ref in sizes)), :]
+    pltpu.make_async_copy(part, part, in_sem.at[2]).wait()
     along_z = dot(rest, common[pl.ds(0, 128), :])
     along_yz = dot(common[pl.ds(256, 4 * N), pl.ds(0, cols)], along_z)
     group = lanes_of(N) // 32
@@ -493,7 +521,7 @@
 
     def wide_copy(k):
         return pltpu.make_async_remote_copy(
-            src_ref=modes.at[i], dst_ref=modes.at[i], send_sem=wide_send.at[k], recv_sem=wide_recv.at[i],
+            src_ref=modes.at[i], dst_ref=modes.at[i], send_sem=wide_send.at[0], recv_sem=wide_recv.at[0],
             device_id=(lax.rem(i + k, W), n), device_id_type=MESH,
         )
 
@@ -501,26 +529,15 @@
         wide_copy(k).start()
         return 0
 
-    def wide_receive(k, _):
-        other = lax.rem(i + k, W)
-        pltpu.make_async_remote_copy(
-            src_ref=modes.at[i], dst_ref=modes.at[other], send_sem=wide_send.at[0], recv_sem=wide_recv.at[other],
-            device_id=(other, n), device_id_type=MESH,
-        ).wait_recv()
-        return 0
-
-    def wide_sent(k, _):
-        wide_copy(k).wait_send()
-        return 0
+    everyone = waiter((W - 1) * (N + 1), wide_send.at[0], wide_recv.at[0], (lax.rem(i + 1, W), n))
 
     lax.fori_loop(1, W, wide_start, 0)
-    start(coarse_far)
-    for pieces in (fine_near, fine_far, middle_w, middle_v, middle_v2):
-        sent(pieces)
+    coarse_far_start()
+    halo_sent()
     for what in range(2):
-        lax.fori_loop(0, N, functools.partial(gather_sent, what), 0)
-    receive(middle_v2)
-    lax.fori_loop(1, W, wide_receive, 0)
+        gather_sent(what)
+    receive(3)
+    everyone.wait_recv()
 
     total = jnp.sum(modes[:, N, :], keepdims=True)
     mean = total * (1.0 / (2 * W * 8 * N * 64))
@@ -555,7 +572,8 @@
         parts.append(part)
     correction = dot(jnp.concatenate(parts, axis=0), common[pl.ds(128, 128), :])
 
-    receive(coarse_far)
+    for d in reach:
+        pl.when(there(-d, 0))(coarse_far_waiter(d).wait_recv)
     u = [gv2[t, window, :] + correction[WINDOW * t : WINDOW * (t + 1), :] for t in range(5)]
 
     def pair_sweep(u, slots):
@@ -629,8 +647,9 @@
         return 0
 
     lax.fori_loop(0, 8, fine_end, 0, unroll=True)
-    sent(coarse_far)
-    lax.fori_loop(1, W, wide_sent, 0)
+    for d in reach:
+        pl.when(there(d, 0))(coarse_far_waiter(d).wait_send)
+    everyone.wait_send()
 
 
 def solution(mesh):
@@ -650,8 +669,8 @@
         vmem((4, 16, 128), F32), vmem((4, 16, 128), F32), vmem((2, 16, 128), F32),
         vmem((5, 2, cols + 16, 128), F32), vmem((5, cols + 16, 128), F32),
         vmem((3, cols + 16, 128), F32), vmem((3, WINDOW, 128), F32),
-        vmem((W, N + 1, 128), F32),
-        dma((5,)), dma((70,)), dma((70,)), dma((2, 3, N)), dma((2, 3, N)), dma((W,)), dma((W,)),
+        vmem((W, N + 1, 128), F32), vmem((640, 128), F32),
+        dma((3,)), dma((8,)), dma((4, 8)), dma((4,)), dma((4,)), dma((2, 3)), dma((2, 3)), dma((1,)), dma((1,)),
     ]
 
     def per_device(divergence, screening):

time: 44 us -> 41.6 us (0.945)
  Pallas kernels: 41.7 us -> 39.2 us
    pallas_call x1, Pallas kernels: 41.7 us -> 39.2 us  [per_device(): pl.pallas_call(functools.partial(cycle_kernel, W, N), out_shape=(block, b...]
where the time goes in v4:
time: 41.6 us; the launch traced here: 41.2 us
  Pallas kernels  39.2 us (94%)
  local copies, waits for them, and re-layouts  1.41 us (3%)
  between operations  0.64 us (2%)
    pallas_call x1, Pallas kernels, per_device(): pl.pallas_call(functools.partial(cycle_kernel, W, N), out_shape=(block, b...  39.2 us
    unnamed x2, local copies, waits for them, and re-layouts  1.41 us

profile of v4, /device:TPU:7, one launch (start us, length us, event | category | flops | bytes accessed | tf_op | source)
XLA Modules:
  0.0 41.2 jit_solution(2915799955193937497)
XLA Ops:
  0.6 39.2 %shard_map.68 = (f32[8,32,256]{2,1,0:T(8,128)S(1)}, f32[8,32,256]{2,1,0:T(8,128)S(1)}) custom-call(f32[8,32,256]{2,1,0:T(8,128)} %f_hbm.1, f32[8,32,256]{2,1,0:T(8,128)} %s_hbm.1, f32[296,128]{1,0:T(8,128)} %constant.6.clone.common_hbm, f32[36,32,128]{2,1,0:T(8,128)} %constant.7.clone.invx_hbm, f32[8,96,128]{2,1,0:T(8,128)} %constant.8.clone.invy_hbm), custom_call_target="tpu_custom_call" | custom-call | tf_op jit(solution)/shard_map/pallas_call | solution.py:678
  39.8 0.7 %copy.9 = f32[8,32,256]{2,1,0:T(8,128)} copy(f32[8,32,256]{2,1,0:T(8,128)S(1)} %get-tuple-element.2) | data formatting | bytes 524288
  40.5 0.7 %copy.10 = f32[8,32,256]{2,1,0:T(8,128)} copy(f32[8,32,256]{2,1,0:T(8,128)S(1)} %get-tuple-element.3) | data formatting | bytes 524288

commit v5 on v4

--- a/solution.py
+++ b/solution.py
@@ -157,46 +157,29 @@
             terms.append(n >= -dy)
         return functools.reduce(jnp.logical_and, terms)
 
+    def flipped(index, mask):
+        result, bit = index, 1
+        while bit <= mask:
+            if mask & bit:
+                result = result + bit * (1 - 2 * lax.rem(lax.div(index, bit), 2))
+            bit *= 2
+        return result
+
+    far_columns = sorted(range(1, N), key=lambda m: (m // 4, min(m % 4, 4 - m % 4), m), reverse=True)
+    far_rows = sorted(range(1, W), key=lambda m: (m // 8 + min(m // 2 % 4, 4 - m // 2 % 4), m), reverse=True)
+    for m in far_columns:
+        other = flipped(n, m)
+        pl.when(has_low)(functools.partial(greet, i - 1, other))
+        pl.when(has_high)(functools.partial(greet, i + 1, other))
+        greet(i, other)
+    for m in far_rows:
+        greet(flipped(i, m), n)
+
+    for load in loads:
+        load.start()
+
     sides = (-1, 1)
     corners = [(dx, dy) for dx in sides for dy in sides]
-    for dx, dy in [(0, -1), (0, 1)] + corners + [(-1, 0), (1, 0)]:
-        pl.when(there(dx, dy))(functools.partial(greet, i + dx, n + dy))
-
-    for load in loads:
-        load.start()
-
-    def greet_narrow(k, _):
-        other = lax.rem(n + k, N)
-
-        @pl.when(jnp.logical_and(other != n - 1, other != n + 1))
-        def _():
-            greet_column(other)
-
-        return 0
-
-    def greet_column(other):
-        greet(i, other)
-
-        @pl.when(has_low)
-        def _():
-            greet(i - 1, other)
-
-        @pl.when(has_high)
-        def _():
-            greet(i + 1, other)
-
-    lax.fori_loop(1, N, greet_narrow, 0)
-
-    def greet_wide(k, _):
-        other = lax.rem(i + k, W)
-
-        @pl.when(jnp.logical_and(other != i - 1, other != i + 1))
-        def _():
-            greet(other, n)
-
-        return 0
-
-    lax.fori_loop(1, W, greet_wide, 0)
 
     def zero(ref, *index):
         shape = ref.at[index].shape if index else ref.shape
@@ -652,6 +635,16 @@
     everyone.wait_send()
 
 
+def store_kernel(out_v, res_v, out_hbm, res_hbm, sem):
+    copies = [
+        pltpu.make_async_copy(src, dst, sem.at[k]) for k, (src, dst) in enumerate(((out_v, out_hbm), (res_v, res_hbm)))
+    ]
+    for copy in copies:
+        copy.start()
+    for copy in copies:
+        copy.wait()
+
+
 def solution(mesh):
     W, N = mesh.shape["wide"], mesh.shape["narrow"]
     common, invx, invy = tables(W, N)
@@ -675,7 +668,7 @@
 
     def per_device(divergence, screening):
         block = pltpu.VMEM((8, 32, 256), F32)
-        return pl.pallas_call(
+        results = pl.pallas_call(
             functools.partial(cycle_kernel, W, N),
             out_shape=(block, block),
             in_specs=[pl.BlockSpec(memory_space=pltpu.HBM)] * 5,
@@ -685,6 +678,16 @@
                 collective_id=0, has_side_effects=True, vmem_limit_bytes=56 * 1024 * 1024
             ),
         )(divergence, screening, jnp.asarray(common), jnp.asarray(invx), jnp.asarray(invy))
+        stored = jax.ShapeDtypeStruct((8, 32, 256), F32)
+        anywhere = pl.BlockSpec(memory_space=pl.ANY)
+        return pl.pallas_call(
+            store_kernel,
+            out_shape=(stored, stored),
+            in_specs=[pl.BlockSpec(memory_space=pltpu.VMEM)] * 2,
+            out_specs=(anywhere, anywhere),
+            scratch_shapes=[dma((2,))],
+            compiler_params=pltpu.CompilerParams(vmem_limit_bytes=4 * 1024 * 1024),
+        )(*results)
 
     spec = P("wide", "narrow", None)
     return jax.shard_map(

time: 41.6 us -> 40.7 us (0.978)
  local copies, waits for them, and re-layouts: 1.41 us -> 0 us
  Pallas kernels: 39.2 us -> 39.7 us
    unnamed x2 -> x0, local copies, waits for them, and re-layouts: 1.41 us -> none
    pallas_call x0 -> x1, Pallas kernels: none -> 0.81 us  [per_device(): pl.pallas_call(store_kernel, out_shape=(stored, stored), in_specs=[pl.Blo...]
where the time goes in v5:
time: 40.7 us; the launch traced here: 40.4 us
  Pallas kernels  39.7 us (98%)
  between operations  0.64 us (2%)
    pallas_call x1, Pallas kernels, per_device(): pl.pallas_call(functools.partial(cycle_kernel, W, N), out_shape=(block, b...  38.9 us

profile of v5, /device:TPU:7, one launch (start us, length us, event | category | flops | bytes accessed | tf_op | source)
XLA Modules:
  0.0 40.4 jit_solution(2577732869880954465)
XLA Ops:
  0.6 38.9 %shard_map.68 = (f32[8,32,256]{2,1,0:T(8,128)S(1)}, f32[8,32,256]{2,1,0:T(8,128)S(1)}) custom-call(f32[8,32,256]{2,1,0:T(8,128)} %f_hbm.1, f32[8,32,256]{2,1,0:T(8,128)} %s_hbm.1, f32[296,128]{1,0:T(8,128)} %constant.6.clone.common_hbm, f32[36,32,128]{2,1,0:T(8,128)} %constant.7.clone.invx_hbm, f32[8,96,128]{2,1,0:T(8,128)} %constant.8.clone.invy_hbm), custom_call_target="tpu_custom_call" | custom-call | tf_op jit(solution)/shard_map/pallas_call | solution.py:671
  39.6 0.8 %shard_map.69 = (f32[8,32,256]{2,1,0:T(8,128)}, f32[8,32,256]{2,1,0:T(8,128)}) custom-call(f32[8,32,256]{2,1,0:T(8,128)S(1)} %get-tuple-element.4.out_v, f32[8,32,256]{2,1,0:T(8,128)S(1)} %get-tuple-element.5.res_v), custom_call_target="tpu_custom_call" | custom-call | tf_op jit(solution)/shard_map/pallas_call | solution.py:683

commit v6 on v5

--- a/solution.py
+++ b/solution.py
@@ -250,8 +250,15 @@
 
     lax.fori_loop(0, 8, start_fine, 0, unroll=True)
 
-    directions = [(0, -1), (0, 1)] + corners + [(-1, 0), (1, 0)]
     rows_of = {}
+    both_x, both_y = jnp.logical_and(has_low, has_high), jnp.logical_and(n > 0, n < N - 1)
+
+    def by_place(call):
+        for sides_x in (1, 2):
+            for sides_y in (1, 2):
+                here_x = both_x if sides_x == 2 else jnp.logical_not(both_x)
+                here_y = both_y if sides_y == 2 else jnp.logical_not(both_y)
+                pl.when(jnp.logical_and(here_x, here_y))(functools.partial(call, sides_x, sides_y))
 
     def waiter(rows, send, recv, to):
         part = tally.at[pl.ds(0, rows), :]
@@ -272,13 +279,23 @@
         return pl.ds(first + low - 1, count), pl.ds(first + size + low - 1, count)
 
     def exchange(family, src, dst, dx, dy):
-        d = directions.index((dx, dy))
-        rows_of[family, d] = rows_of.get((family, d), 0) + int(np.prod(src.shape)) // 128
+        kind = (family, dx != 0, dy != 0)
+        if dx >= 0 and dy >= 0:
+            rows_of[kind] = rows_of.get(kind, 0) + int(np.prod(src.shape)) // 128
         copy = pltpu.make_async_remote_copy(
-            src_ref=src, dst_ref=dst, send_sem=send_sem.at[d], recv_sem=recv_sem.at[family, d],
+            src_ref=src, dst_ref=dst, send_sem=send_sem.at[0], recv_sem=recv_sem.at[family],
             device_id=beside(dx, dy), device_id_type=MESH,
         )
         return copy, there(dx, dy)
+
+    def halo_waiter(families, sides_x, sides_y):
+        rows = sum(
+            sides_x * rows_of[family, True, False]
+            + sides_y * rows_of[family, False, True]
+            + sides_x * sides_y * rows_of[family, True, True]
+            for family in families
+        )
+        return waiter(rows, send_sem.at[0], recv_sem.at[families[0]], (lax.rem(i + 1, W), n))
 
     def fine_piece(family, ref, dx, dy, depth_x=None, depth_y=None):
         src_x, dst_x = span(dx, 4, 8, depth_x)
@@ -295,14 +312,10 @@
             pl.when(to)(copy.start)
 
     def receive(family):
-        for d, (dx, dy) in enumerate(directions):
-            arrival = waiter(rows_of[family, d], send_sem.at[d], recv_sem.at[family, d], beside(dx, dy))
-            pl.when(there(-dx, -dy))(arrival.wait_recv)
+        by_place(lambda sides_x, sides_y: halo_waiter([family], sides_x, sides_y).wait_recv())
 
     def halo_sent():
-        for d, (dx, dy) in enumerate(directions):
-            rows = sum(rows_of[family, d] for family in range(4))
-            pl.when(there(dx, dy))(waiter(rows, send_sem.at[d], recv_sem.at[0, d], beside(dx, dy)).wait_send)
+        by_place(lambda sides_x, sides_y: halo_waiter(range(3), sides_x, sides_y).wait_send())
 
     fine_near = (
         [fine_piece(0, va, 0, d, None, (1, 2)) for d in sides]
@@ -330,15 +343,14 @@
 
     middle_w = middle_pieces(2, wb, 3, 2)
     middle_v = middle_pieces(2, vb, 3, 2)
-    middle_v2 = middle_pieces(3, v2b, 4, 3)
+    middle_v2 = middle_pieces(1, v2b, 4, 3)
 
     window = pl.ds(pl.multiple_of(8 * n, 8), WINDOW)
     reach = (-2, -1, 1, 2)
 
     def coarse_far(d):
-        k = reach.index(d)
         args = dict(
-            send_sem=far_send.at[k], recv_sem=far_recv.at[k], device_id=beside(d, 0), device_id_type=MESH
+            send_sem=far_send.at[0], recv_sem=far_recv.at[0], device_id=beside(d, 0), device_id_type=MESH
         )
         copies = [pltpu.make_async_remote_copy(src_ref=gv2.at[2, window, :], dst_ref=gv2.at[2 - d, window, :], **args)]
         if abs(d) == 2:
@@ -354,9 +366,16 @@
             for copy in coarse_far(d):
                 pl.when(there(d, 0))(copy.start)
 
-    def coarse_far_waiter(d):
-        k = reach.index(d)
-        return waiter((3 if abs(d) == 2 else 1) * WINDOW, far_send.at[k], far_recv.at[k], beside(d, 0))
+    def far_wait(call):
+        further = jnp.logical_and(i > 1, i < W - 2)
+        cases = (
+            (1, 1, jnp.logical_not(both_x)),
+            (2, 1, jnp.logical_and(both_x, jnp.logical_not(further))),
+            (2, 2, further),
+        )
+        for near, far, here in cases:
+            rows = (near + 3 * far) * WINDOW
+            pl.when(here)(functools.partial(call, waiter(rows, far_send.at[0], far_recv.at[0], beside(1, 0))))
 
     greeted = (W - 1) + (N - 1) * (1 + has_low.astype(jnp.int32) + has_high.astype(jnp.int32))
     pl.semaphore_wait(barrier, greeted)
@@ -391,14 +410,15 @@
         target = lax.rem(i + dx + W, W)
         return pltpu.make_async_remote_copy(
             src_ref=gvw.at[2, what, own_cols, :], dst_ref=gvw.at[2 - dx, what, own_cols, :],
-            send_sem=gather_send.at[what, dx + 1], recv_sem=gather_recv.at[what, 1 - dx],
+            send_sem=gather_send.at[0], recv_sem=gather_recv.at[0],
             device_id=(target, other), device_id_type=MESH,
         )
 
-    def gather_waiter(what, dx):
-        rows = 8 * (N if dx else N - 1)
-        target = (lax.rem(i + 1, W), n)
-        return waiter(rows, gather_send.at[what, dx + 1], gather_recv.at[what, dx + 1], target)
+    def gather_wait(call):
+        for sides_x, here in ((2, both_x), (1, jnp.logical_not(both_x))):
+            rows = 2 * 8 * (N - 1 + sides_x * N)
+            target = (lax.rem(i + 1, W), n)
+            pl.when(here)(functools.partial(call, waiter(rows, gather_send.at[0], gather_recv.at[0], target)))
 
     def for_each(k, call):
         pl.when(k > 0)(functools.partial(call, 0))
@@ -409,12 +429,6 @@
         for_each(k, lambda dx: gather_copy(what, dx, k).start())
         return 0
 
-    def gather_receive(what):
-        for_each(1, lambda dx: gather_waiter(what, dx).wait_recv())
-
-    def gather_sent(what):
-        for_each(1, lambda dx: gather_waiter(what, dx).wait_send())
-
     lax.fori_loop(0, N, functools.partial(gather_start, 1), 0)
 
     def fine_v2(a, count, r, _):
@@ -423,35 +437,38 @@
             v2a[r, h, pl.ds(a, count), :] = (1.0 + KEEP) * centre[h] + wa[r, h, pl.ds(a, count), :] * summed[h]
         return 0
 
+    def fine_down(a, count, q, _):
+        cells = pl.ds(a - 8, count)
+        sums = [fine_sum(v2a, 2 * q + k + 4, a, count) for k in range(2)]
+        for h in range(2):
+            lanes = pl.ds(128 * h, 128)
+            rest = [
+                f_in[2 * q + k, cells, lanes] - (6.0 + s_in[2 * q + k, cells, lanes]) * centre[h] + summed[h]
+                for k, (centre, summed) in enumerate(sums)
+            ]
+            fold[q, h, cells, :] = rest[0] + rest[1]
+        low, high = (
+            fold[q, h, pl.ds(a - 8, count // 2, stride=2), :] + fold[q, h, pl.ds(a - 7, count // 2, stride=2), :]
+            for h in range(2)
+        )
+        source = 0.5 * fold_lanes(low, high)
+        fb[q, pl.ds((a - 8) // 2, count // 2), :] = source
+        part = (q + 4, pl.ds(4 + a // 2, count // 2), slice(None))
+        vb[part] = source * wb[part]
+        return 0
+
+    def fine_level(v2_a, v2_count, outer_a, outer_count, a, count):
+        for r in (3, 12):
+            fine_v2(outer_a, outer_count, r, 0)
+        lax.fori_loop(4, 12, functools.partial(fine_v2, v2_a, v2_count), 0, unroll=True)
+        lax.fori_loop(0, 4, functools.partial(fine_down, a, count), 0, unroll=True)
+
     receive(0)
-    fine_v2(8, 32, 3, 0)
-    lax.fori_loop(4, 12, functools.partial(fine_v2, 7, 34), 0, unroll=True)
-    fine_v2(8, 32, 12, 0)
-
-    def fine_residual(ref, r, h, centre, summed):
-        lanes = pl.ds(128 * h, 128)
-        return f_in[r, :, lanes] - (6.0 + s_in[r, :, lanes]) * centre + summed
-
-    def fine_down(q, _):
-        c0, n0 = fine_sum(v2a, 2 * q + 4, 8, 32)
-        c1, n1 = fine_sum(v2a, 2 * q + 5, 8, 32)
-        for h in range(2):
-            fold[q, h, :, :] = fine_residual(v2a, 2 * q, h, c0[h], n0[h]) + fine_residual(
-                v2a, 2 * q + 1, h, c1[h], n1[h]
-            )
-        low, high = (
-            fold[q, h, pl.ds(0, 16, stride=2), :] + fold[q, h, pl.ds(1, 16, stride=2), :] for h in range(2)
-        )
-        source = 0.5 * fold_lanes(low, high)
-        fb[q, :, :] = source
-        vb[q + 4, pl.ds(8, 16), :] = source * wb[q + 4, pl.ds(8, 16), :]
-        return 0
-
-    lax.fori_loop(0, 4, fine_down, 0, unroll=True)
-    start(middle_v)
-
-    receive(1)
-    lax.fori_loop(1, 15, functools.partial(fine_v2, 4, 40), 0, unroll=True)
+    fine_level(7, 8, 8, 7, 8, 6)
+    fine_level(33, 8, 33, 7, 34, 6)
+    start(middle_v[:6])
+    fine_level(15, 18, 15, 18, 14, 20)
+    start(middle_v[6:])
 
     receive(2)
     for r in range(3, 9):
@@ -470,8 +487,7 @@
 
     lax.fori_loop(0, N, functools.partial(gather_start, 0), 0)
     start(middle_v2)
-    gather_receive(1)
-    gather_receive(0)
+    gather_wait(lambda copies: copies.wait_recv())
 
     slab = pl.ds(8, cols)
     turned = [rolled(gvw[t, 0, slab, :], 64, 1) for t in (1, 2, 3)]
@@ -517,9 +533,10 @@
     lax.fori_loop(1, W, wide_start, 0)
     coarse_far_start()
     halo_sent()
-    for what in range(2):
-        gather_sent(what)
-    receive(3)
+    gather_wait(lambda copies: copies.wait_send())
+
+    receive(1)
+    lax.fori_loop(1, 15, functools.partial(fine_v2, 4, 40), 0, unroll=True)
     everyone.wait_recv()
 
     total = jnp.sum(modes[:, N, :], keepdims=True)
@@ -555,8 +572,7 @@
         parts.append(part)
     correction = dot(jnp.concatenate(parts, axis=0), common[pl.ds(128, 128), :])
 
-    for d in reach:
-        pl.when(there(-d, 0))(coarse_far_waiter(d).wait_recv)
+    far_wait(lambda copies: copies.wait_recv())
     u = [gv2[t, window, :] + correction[WINDOW * t : WINDOW * (t + 1), :] for t in range(5)]
 
     def pair_sweep(u, slots):
@@ -626,12 +642,11 @@
         for h in range(2):
             lanes = pl.ds(128 * h, 128)
             out_v[r, :, lanes] = centre[h]
-            res_v[r, :, lanes] = fine_residual(ua, r, h, centre[h], summed[h])
+            res_v[r, :, lanes] = f_in[r, :, lanes] - (6.0 + s_in[r, :, lanes]) * centre[h] + summed[h]
         return 0
 
     lax.fori_loop(0, 8, fine_end, 0, unroll=True)
-    for d in reach:
-        pl.when(there(d, 0))(coarse_far_waiter(d).wait_send)
+    far_wait(lambda copies: copies.wait_send())
     everyone.wait_send()
 
 
@@ -662,8 +677,8 @@
         vmem((4, 16, 128), F32), vmem((4, 16, 128), F32), vmem((2, 16, 128), F32),
         vmem((5, 2, cols + 16, 128), F32), vmem((5, cols + 16, 128), F32),
         vmem((3, cols + 16, 128), F32), vmem((3, WINDOW, 128), F32),
-        vmem((W, N + 1, 128), F32), vmem((640, 128), F32),
-        dma((3,)), dma((8,)), dma((4, 8)), dma((4,)), dma((4,)), dma((2, 3)), dma((2, 3)), dma((1,)), dma((1,)),
+        vmem((W, N + 1, 128), F32), vmem((2048, 128), F32),
+        dma((3,)), dma((1,)), dma((3,)), dma((1,)), dma((1,)), dma((1,)), dma((1,)), dma((1,)), dma((1,)),
     ]
 
     def per_device(divergence, screening):

time: 40.7 us -> 39.9 us (0.980)
  Pallas kernels: 39.7 us -> 39.1 us
    pallas_call x1, Pallas kernels: 38.9 us -> 38.3 us  [per_device(): pl.pallas_call(functools.partial(cycle_kernel, W, N), out_shape=(block, b...]
where the time goes in v6:
time: 39.9 us; the launch traced here: 39.8 us
  Pallas kernels  39.1 us (98%)
  between operations  0.64 us (2%)
    pallas_call x1, Pallas kernels, per_device(): pl.pallas_call(functools.partial(cycle_kernel, W, N), out_shape=(block, b...  38.3 us
    pallas_call x1, Pallas kernels, per_device(): pl.pallas_call(store_kernel, out_shape=(stored, stored), in_specs=[pl.Blo...  0.81 us

profile of v6, /device:TPU:7, one launch (start us, length us, event | category | flops | bytes accessed | tf_op | source)
XLA Modules:
  0.0 39.8 jit_solution(3252924191227444025)
XLA Ops:
  0.6 38.3 %shard_map.68 = (f32[8,32,256]{2,1,0:T(8,128)S(1)}, f32[8,32,256]{2,1,0:T(8,128)S(1)}) custom-call(f32[8,32,256]{2,1,0:T(8,128)} %f_hbm.1, f32[8,32,256]{2,1,0:T(8,128)} %s_hbm.1, f32[296,128]{1,0:T(8,128)} %constant.6.clone.common_hbm, f32[36,32,128]{2,1,0:T(8,128)} %constant.7.clone.invx_hbm, f32[8,96,128]{2,1,0:T(8,128)} %constant.8.clone.invy_hbm), custom_call_target="tpu_custom_call" | custom-call | tf_op jit(solution)/shard_map/pallas_call | solution.py:686
  39.0 0.8 %shard_map.69 = (f32[8,32,256]{2,1,0:T(8,128)}, f32[8,32,256]{2,1,0:T(8,128)}) custom-call(f32[8,32,256]{2,1,0:T(8,128)S(1)} %get-tuple-element.4.out_v, f32[8,32,256]{2,1,0:T(8,128)S(1)} %get-tuple-element.5.res_v), custom_call_target="tpu_custom_call" | custom-call | tf_op jit(solution)/shard_map/pallas_call | solution.py:698

commit v7 on v6

--- a/solution.py
+++ b/solution.py
@@ -189,7 +189,7 @@
 
     @pl.when(i == 0)
     def _():
-        for ref in (va, wa):
+        for ref in (va, wa, v2a):
             zero(ref, pl.ds(0, 4))
         for ref in (vb, wb, v2b):
             zero(ref, pl.ds(0, 4))
@@ -198,7 +198,7 @@
 
     @pl.when(i == W - 1)
     def _():
-        for ref in (va, wa):
+        for ref in (va, wa, v2a):
             zero(ref, pl.ds(12, 4))
         for ref in (vb, wb, v2b):
             zero(ref, pl.ds(8, 4))
@@ -217,14 +217,14 @@
 
     @pl.when(n == 0)
     def _():
-        for ref in (va, wa):
+        for ref in (va, wa, v2a):
             zero(ref, all_, all_, pl.ds(0, 8))
         for ref in (vb, wb, v2b):
             zero(ref, all_, pl.ds(0, 8))
 
     @pl.when(n == N - 1)
     def _():
-        for ref in (va, wa):
+        for ref in (va, wa, v2a):
             zero(ref, all_, all_, pl.ds(40, 8))
         for ref in (vb, wb, v2b):
             zero(ref, all_, pl.ds(24, 8))
@@ -325,13 +325,13 @@
         + [fine_piece(0, wa, d, 0, (1, 1)) for d in sides]
     )
     fine_far = (
-        [fine_piece(1, va, 0, d, None, (3, 4)) for d in sides]
-        + [fine_piece(1, wa, 0, d, None, (2, 3)) for d in sides]
-        + [fine_piece(1, va, dx, dy, (1, 1), (2, 3)) for dx, dy in corners]
-        + [fine_piece(1, va, dx, dy, (2, 3), (1, 2)) for dx, dy in corners]
-        + [fine_piece(1, wa, dx, dy, (1, 2), (1, 2)) for dx, dy in corners]
-        + [fine_piece(1, va, d, 0, (3, 4)) for d in sides]
-        + [fine_piece(1, wa, d, 0, (2, 3)) for d in sides]
+        [fine_piece(1, v2a, 0, d, None, (2, 3)) for d in sides]
+        + [fine_piece(1, wa, 0, d, None, (2, 2)) for d in sides]
+        + [fine_piece(1, v2a, dx, dy, (1, 1), (1, 2)) for dx, dy in corners]
+        + [fine_piece(1, v2a, dx, dy, (2, 2), (1, 1)) for dx, dy in corners]
+        + [fine_piece(1, wa, dx, dy, (1, 1), (1, 1)) for dx, dy in corners]
+        + [fine_piece(1, v2a, d, 0, (2, 3)) for d in sides]
+        + [fine_piece(1, wa, d, 0, (2, 2)) for d in sides]
     )
 
     def middle_pieces(family, ref, depth, corner):
@@ -381,7 +381,6 @@
     pl.semaphore_wait(barrier, greeted)
 
     start(fine_near)
-    start(fine_far)
 
     def screen_middle(q, _):
         for h in range(2):
@@ -429,7 +428,6 @@
         for_each(k, lambda dx: gather_copy(what, dx, k).start())
         return 0
 
-    lax.fori_loop(0, N, functools.partial(gather_start, 1), 0)
 
     def fine_v2(a, count, r, _):
         centre, summed = fine_sum(va, r, a, count)
@@ -469,6 +467,8 @@
     start(middle_v[:6])
     fine_level(15, 18, 15, 18, 14, 20)
     start(middle_v[6:])
+    start(fine_far)
+    lax.fori_loop(0, N, functools.partial(gather_start, 1), 0)
 
     receive(2)
     for r in range(3, 9):
@@ -536,7 +536,6 @@
     gather_wait(lambda copies: copies.wait_send())
 
     receive(1)
-    lax.fori_loop(1, 15, functools.partial(fine_v2, 4, 40), 0, unroll=True)
     everyone.wait_recv()
 
     total = jnp.sum(modes[:, N, :], keepdims=True)

time: 39.9 us -> 38.7 us (0.970)
  Pallas kernels: 39.1 us -> 38 us
    pallas_call x1, Pallas kernels: 38.3 us -> 37.2 us  [per_device(): pl.pallas_call(functools.partial(cycle_kernel, W, N), out_shape=(block, b...]
where the time goes in v7:
time: 38.7 us; the launch traced here: 38.6 us
  Pallas kernels  38 us (98%)
  between operations  0.64 us (2%)
    pallas_call x1, Pallas kernels, per_device(): pl.pallas_call(functools.partial(cycle_kernel, W, N), out_shape=(block, b...  37.2 us
    pallas_call x1, Pallas kernels, per_device(): pl.pallas_call(store_kernel, out_shape=(stored, stored), in_specs=[pl.Blo...  0.81 us

profile of v7, /device:TPU:7, one launch (start us, length us, event | category | flops | bytes accessed | tf_op | source)
XLA Modules:
  0.0 38.6 jit_solution(3619482547580519337)
XLA Ops:
  0.6 37.2 %shard_map.68 = (f32[8,32,256]{2,1,0:T(8,128)S(1)}, f32[8,32,256]{2,1,0:T(8,128)S(1)}) custom-call(f32[8,32,256]{2,1,0:T(8,128)} %f_hbm.1, f32[8,32,256]{2,1,0:T(8,128)} %s_hbm.1, f32[296,128]{1,0:T(8,128)} %constant.6.clone.common_hbm, f32[36,32,128]{2,1,0:T(8,128)} %constant.7.clone.invx_hbm, f32[8,96,128]{2,1,0:T(8,128)} %constant.8.clone.invy_hbm), custom_call_target="tpu_custom_call" | custom-call | tf_op jit(solution)/shard_map/pallas_call | solution.py:685
  37.8 0.8 %shard_map.69 = (f32[8,32,256]{2,1,0:T(8,128)}, f32[8,32,256]{2,1,0:T(8,128)}) custom-call(f32[8,32,256]{2,1,0:T(8,128)S(1)} %get-tuple-element.4.out_v, f32[8,32,256]{2,1,0:T(8,128)S(1)} %get-tuple-element.5.res_v), custom_call_target="tpu_custom_call" | custom-call | tf_op jit(solution)/shard_map/pallas_call | solution.py:697

commit v8 on v7

--- a/solution.py
+++ b/solution.py
@@ -130,8 +130,8 @@
         pltpu.make_async_copy(src, dst, in_sem.at[min(k, 2)])
         for k, (src, dst) in enumerate(
             (
-                (s_hbm, s_in),
-                (f_hbm, f_in),
+                (s_hbm, s_in.at[:, pl.ds(0, 32), :]),
+                (f_hbm, f_in.at[:, pl.ds(0, 32), :]),
                 (common_hbm, common),
                 (invx_hbm.at[pl.ds(i, 5)], invx),
                 (invy_hbm.at[n], invy),
@@ -242,10 +242,10 @@
 
     def start_fine(r, _):
         for h in range(2):
-            screen = s_in[r, :, pl.ds(128 * h, 128)]
+            screen = s_in[r, pl.ds(0, 32), pl.ds(128 * h, 128)]
             weight = OMEGA / (6.0 + screen)
             wa[r + 4, h, pl.ds(8, 32), :] = weight
-            va[r + 4, h, pl.ds(8, 32), :] = f_in[r, :, pl.ds(128 * h, 128)] * weight
+            va[r + 4, h, pl.ds(8, 32), :] = f_in[r, pl.ds(0, 32), pl.ds(128 * h, 128)] * weight
         return 0
 
     lax.fori_loop(0, 8, start_fine, 0, unroll=True)
@@ -385,7 +385,7 @@
     def screen_middle(q, _):
         for h in range(2):
             lanes = pl.ds(128 * h, 128)
-            fold[q, h, :, :] = s_in[2 * q, :, lanes] + s_in[2 * q + 1, :, lanes]
+            fold[q, h, pl.ds(0, 32), :] = s_in[2 * q, pl.ds(0, 32), lanes] + s_in[2 * q + 1, pl.ds(0, 32), lanes]
         low, high = (
             fold[q, h, pl.ds(0, 16, stride=2), :] + fold[q, h, pl.ds(1, 16, stride=2), :] for h in range(2)
         )
@@ -477,7 +477,7 @@
     for r in range(4):
         centre, summed = middle_sum(tb, r + 4, 8, 16)
         v2b[r + 4, pl.ds(8, 16), :] = centre
-        rest = fb[r, :, :] - db[r, :, :] * centre + summed
+        rest = fb[r, pl.ds(0, 16), :] - db[r, :, :] * centre + summed
         if r % 2 == 0:
             held = rest
         else:
@@ -641,7 +641,7 @@
         for h in range(2):
             lanes = pl.ds(128 * h, 128)
             out_v[r, :, lanes] = centre[h]
-            res_v[r, :, lanes] = f_in[r, :, lanes] - (6.0 + s_in[r, :, lanes]) * centre[h] + summed[h]
+            res_v[r, :, lanes] = f_in[r, pl.ds(0, 32), lanes] - (6.0 + s_in[r, pl.ds(0, 32), lanes]) * centre[h] + summed[h]
         return 0
 
     lax.fori_loop(0, 8, fine_end, 0, unroll=True)
@@ -667,13 +667,13 @@
     dma = pltpu.SemaphoreType.DMA
     fine, middle = (16, 2, 48, 128), (12, 32, 128)
     scratch = [
-        vmem((8, 32, 256), F32), vmem((8, 32, 256), F32),
+        vmem((8, 40, 256), F32), vmem((8, 40, 256), F32),
         vmem(common.shape, F32), vmem((5, W, 128), F32), vmem((4 * WINDOW, 128), F32),
         vmem(fine, F32), vmem(fine, F32), vmem(fine, F32), vmem(fine, F32), vmem(fine, F32),
-        vmem((4, 2, 32, 128), F32),
+        vmem((4, 2, 48, 128), F32),
         vmem(middle, F32), vmem(middle, F32), vmem(middle, F32), vmem(middle, F32),
         vmem(middle, F32), vmem(middle, F32),
-        vmem((4, 16, 128), F32), vmem((4, 16, 128), F32), vmem((2, 16, 128), F32),
+        vmem((4, 24, 128), F32), vmem((4, 16, 128), F32), vmem((2, 16, 128), F32),
         vmem((5, 2, cols + 16, 128), F32), vmem((5, cols + 16, 128), F32),
         vmem((3, cols + 16, 128), F32), vmem((3, WINDOW, 128), F32),
         vmem((W, N + 1, 128), F32), vmem((2048, 128), F32),

time: 38.7 us -> 38.7 us (level)
  no operation moved by 1% of the time
where the time goes in v8:
time: 38.7 us; the launch traced here: 38.6 us
  Pallas kernels  38 us (98%)
  between operations  0.64 us (2%)
    pallas_call x1, Pallas kernels, per_device(): pl.pallas_call(functools.partial(cycle_kernel, W, N), out_shape=(block, b...  37.2 us
    pallas_call x1, Pallas kernels, per_device(): pl.pallas_call(store_kernel, out_shape=(stored, stored), in_specs=[pl.Blo...  0.81 us

profile of v8, /device:TPU:7, one launch (start us, length us, event | category | flops | bytes accessed | tf_op | source)
XLA Modules:
  0.0 38.6 jit_solution(500005532782907492)
XLA Ops:
  0.6 37.2 %shard_map.68 = (f32[8,32,256]{2,1,0:T(8,128)S(1)}, f32[8,32,256]{2,1,0:T(8,128)S(1)}) custom-call(f32[8,32,256]{2,1,0:T(8,128)} %f_hbm.1, f32[8,32,256]{2,1,0:T(8,128)} %s_hbm.1, f32[296,128]{1,0:T(8,128)} %constant.6.clone.common_hbm, f32[36,32,128]{2,1,0:T(8,128)} %constant.7.clone.invx_hbm, f32[8,96,128]{2,1,0:T(8,128)} %constant.8.clone.invy_hbm), custom_call_target="tpu_custom_call" | custom-call | tf_op jit(solution)/shard_map/pallas_call | solution.py:685
  37.8 0.8 %shard_map.69 = (f32[8,32,256]{2,1,0:T(8,128)}, f32[8,32,256]{2,1,0:T(8,128)}) custom-call(f32[8,32,256]{2,1,0:T(8,128)S(1)} %get-tuple-element.4.out_v, f32[8,32,256]{2,1,0:T(8,128)S(1)} %get-tuple-element.5.res_v), custom_call_target="tpu_custom_call" | custom-call | tf_op jit(solution)/shard_map/pallas_call | solution.py:697

commit v9 on v8

--- a/solution.py
+++ b/solution.py
@@ -327,8 +327,7 @@
     fine_far = (
         [fine_piece(1, v2a, 0, d, None, (2, 3)) for d in sides]
         + [fine_piece(1, wa, 0, d, None, (2, 2)) for d in sides]
-        + [fine_piece(1, v2a, dx, dy, (1, 1), (1, 2)) for dx, dy in corners]
-        + [fine_piece(1, v2a, dx, dy, (2, 2), (1, 1)) for dx, dy in corners]
+        + [fine_piece(1, v2a, dx, dy, (1, 2), (1, 2)) for dx, dy in corners]
         + [fine_piece(1, wa, dx, dy, (1, 1), (1, 1)) for dx, dy in corners]
         + [fine_piece(1, v2a, d, 0, (2, 3)) for d in sides]
         + [fine_piece(1, wa, d, 0, (2, 2)) for d in sides]

time: 38.7 us -> 38.8 us (level)
  no operation moved by 1% of the time
where the time goes in v9:
time: 38.8 us; the launch traced here: 38.6 us
  Pallas kernels  37.9 us (98%)
  between operations  0.64 us (2%)
    pallas_call x1, Pallas kernels, per_device(): pl.pallas_call(functools.partial(cycle_kernel, W, N), out_shape=(block, b...  37.1 us
    pallas_call x1, Pallas kernels, per_device(): pl.pallas_call(store_kernel, out_shape=(stored, stored), in_specs=[pl.Blo...  0.81 us

profile of v9, /device:TPU:7, one launch (start us, length us, event | category | flops | bytes accessed | tf_op | source)
XLA Modules:
  0.0 38.6 jit_solution(14183074659270687296)
XLA Ops:
  0.6 37.1 %shard_map.68 = (f32[8,32,256]{2,1,0:T(8,128)S(1)}, f32[8,32,256]{2,1,0:T(8,128)S(1)}) custom-call(f32[8,32,256]{2,1,0:T(8,128)} %f_hbm.1, f32[8,32,256]{2,1,0:T(8,128)} %s_hbm.1, f32[296,128]{1,0:T(8,128)} %constant.6.clone.common_hbm, f32[36,32,128]{2,1,0:T(8,128)} %constant.7.clone.invx_hbm, f32[8,96,128]{2,1,0:T(8,128)} %constant.8.clone.invy_hbm), custom_call_target="tpu_custom_call" | custom-call | tf_op jit(solution)/shard_map/pallas_call | solution.py:684
  37.7 0.8 %shard_map.69 = (f32[8,32,256]{2,1,0:T(8,128)}, f32[8,32,256]{2,1,0:T(8,128)}) custom-call(f32[8,32,256]{2,1,0:T(8,128)S(1)} %get-tuple-element.4.out_v, f32[8,32,256]{2,1,0:T(8,128)S(1)} %get-tuple-element.5.res_v), custom_call_target="tpu_custom_call" | custom-call | tf_op jit(solution)/shard_map/pallas_call | solution.py:696
